TPU v7x, 32 devices: a whole 2x2x4 slice. The times are simulated.
32 devices in a mesh: dp: 4 (over z), context: 2 (over x), expert: 4 (over y, core).
Axes of the slice: x: 2, y: 2, z: 4, core: 2. Of those that a mesh axis runs over, the one named last changes fastest.
Arguments:
- hidden_in: bfloat16 [16, 1024, 768], P(('dp', 'expert'), 'context'), may hold values from -6 to 6
- prev_logits: float32 [16, 1024, 12], P(('dp', 'expert'), 'context'), may hold values from -6 to 6
- segment_ids: int32 [16, 1024], P(('dp', 'expert'), 'context'), may hold values from 0 to 6, as said below
- routes: int32 [16, 1024, 2], P(('dp', 'expert'), 'context'), may hold values from 0 to 11, as said below
- adapter_ids: int32 [16], replicated, may hold values from 0 to 7
- attn_gain: bfloat16 [768], replicated, may hold values from 0.5 to 1.5
- w_qkv: bfloat16 [768, 2304], replicated, may hold values from -0.21875 to 0.21875
- w_out: bfloat16 [768, 768], replicated, may hold values from -2 to 2
- attn_down: bfloat16 [8, 4, 768, 16], replicated, may hold values from -0.21875 to 0.21875
- attn_up: bfloat16 [8, 4, 16, 768], replicated, may hold values from -0.75 to 0.75
- ffn_gain: bfloat16 [768], replicated, may hold values from 0.5 to 1.5
- router_weight: bfloat16 [768, 12], replicated, may hold values from -0.109375 to 0.109375
- gate_mix: float32 [12, 12], replicated, may hold values from -0.875 to 0.875
- const_mix: bfloat16 [2, 768, 2], replicated, may hold values from -0.21875 to 0.21875
- const_vec: bfloat16 [2, 768], replicated, may hold values from -6 to 6
- w_gate_up: bfloat16 [8, 768, 4096], P('expert'), may hold values from -0.21875 to 0.21875
- w_down: bfloat16 [8, 2048, 768], P('expert'), may hold values from -0.125 to 0.125
- exp_in_down: bfloat16 [8, 8, 768, 32], P(None, 'expert'), may hold values from -0.21875 to 0.21875
- exp_in_up: bfloat16 [8, 8, 2, 16, 2048], P(None, 'expert'), may hold values from -0.75 to 0.75
- exp_out_down: bfloat16 [8, 8, 2048, 16], P(None, 'expert'), may hold values from -0.125 to 0.125
- exp_out_up: bfloat16 [8, 8, 16, 768], P(None, 'expert'), may hold values from -0.75 to 0.75
- cotangent: bfloat16 [16, 1024, 768], P(('dp', 'expert'), 'context'), may hold values from -6 to 6
Outputs:
- hidden_out: bfloat16 [16, 1024, 768], P(('dp', 'expert'), 'context')
- grad_in: float32 [16, 1024, 768], P(('dp', 'expert'), 'context')
- grad_prev: float32 [16, 1024, 12], P(('dp', 'expert'), 'context')
- grad_attn_down: float32 [8, 4, 768, 16], replicated
- grad_attn_up: float32 [8, 4, 16, 768], replicated
- grad_exp_in_down: float32 [8, 8, 768, 32], P(None, 'expert')
- grad_exp_in_up: float32 [8, 8, 2, 16, 2048], P(None, 'expert')
- grad_exp_out_down: float32 [8, 8, 2048, 16], P(None, 'expert')
- grad_exp_out_up: float32 [8, 8, 16, 768], P(None, 'expert')
Inputs may be any that keep to these rules, and one draw needn't show every extreme that they name: `segment_ids`: segment ids never fall along a sequence; all changes of segment lie in a sequence's first 512 and last 512 positions. `routes`: each token names two different kinds: 0 to 7 are FFN experts, 8 the zero expert, 9 the copy expert, 10 and 11 the constant experts. Among the 512 tokens of one device the counts of the 12 kinds are, in some order, 8, 8, 7, 6, 6, 5, 5, 4, 4, 4, 4, 3 times 512 // 32, so no kind is named more than 512 // 4 times; among the devices that share their dp and context indices, one FFN expert is named exactly 512 // 4 times on each.
All inputs are finite; a program needn't handle non-finite values.
Results may differ from a plain program's by a relative error of at most 0.017.
The roundings to bfloat16 on the way count: a program that leaves them out, or rounds other values in their place, can miss the bound.
Values may be sent and summed in bfloat16 or wider, within the bound.
A program may use at most 256 MiB of HBM per device.

v0:
```python
import math

import jax
import jax.numpy as jnp
from jax import lax
from jax.sharding import PartitionSpec as P

HEADS = 12


EPSILON = 1e-06
ADAPT_SCALE = 2.0
NEG = -1e30
HIGH = lax.Precision.HIGHEST


def rotate(vectors, positions, direction):
    half_dim = vectors.shape[-1] // 2
    frequency = jnp.exp(
        jnp.arange(half_dim).astype(jnp.float32) * (-2.0 * math.log(10000.0) / vectors.shape[-1])
    )
    angles = positions[:, None] * frequency[None, :]
    cosine = jnp.cos(angles)[:, None, :]
    sine_part = direction * jnp.sin(angles)[:, None, :]
    first_half = vectors[..., :half_dim]
    second_half = vectors[..., half_dim:]
    return jnp.concatenate(
        [
            first_half * cosine - second_half * sine_part,
            first_half * sine_part + second_half * cosine,
        ],
        -1,
    )


def bdot(form, left, right):
    return jnp.einsum(form, left, right, preferred_element_type=jnp.float32)


def fdot(form, left, right):
    return jnp.einsum(form, left, right, precision=HIGH, preferred_element_type=jnp.float32)


def masked_scores(queries, key_rows, query_pos, query_seg, key_pos, key_seg):
    raw_scores = bdot("qhd,khd->hqk", queries, key_rows) * queries.shape[-1] ** (-0.5)
    allowed = (query_seg[:, None] == key_seg[None, :]) & (key_pos[None, :] <= query_pos[:, None])
    return jnp.where(allowed[None], raw_scores, NEG)


def block_grads(
    queries,
    d_out,
    log_total,
    row_delta,
    query_pos,
    query_seg,
    key_rows,
    value_rows,
    key_pos,
    key_seg,
):
    probs_block = jnp.exp(
        masked_scores(queries, key_rows, query_pos, query_seg, key_pos, key_seg)
        - log_total[:, :, None]
    )
    rounded = probs_block.astype(jnp.bfloat16)
    d_probs = bdot("qhd,khd->hqk", d_out, value_rows)
    d_scores = (probs_block * (d_probs - row_delta[:, :, None])).astype(jnp.bfloat16)
    score_scale = queries.shape[-1] ** (-0.5)
    d_query = bdot("hqk,khd->qhd", d_scores, key_rows) * score_scale
    d_key = bdot("hqk,qhd->khd", d_scores, queries) * score_scale
    d_value = bdot("hqk,qhd->khd", rounded, d_out)
    return (d_query, d_key, d_value)


def expert_hidden(arrived, tables, w_gate_up, ffn_width):
    rank_dim = tables[1].shape[3]
    joined_rows = bdot("jecd,edf->jecf", arrived, w_gate_up)
    rank_in = bdot("jecd,jedr->jecr", arrived, tables[0]).astype(jnp.bfloat16)
    gate_pre = joined_rows[..., :ffn_width] + ADAPT_SCALE * bdot(
        "jecr,jerf->jecf", rank_in[..., :rank_dim], tables[1][:, :, 0]
    )
    up_pre = joined_rows[..., ffn_width:] + ADAPT_SCALE * bdot(
        "jecr,jerf->jecf", rank_in[..., rank_dim:], tables[1][:, :, 1]
    )
    return (gate_pre, up_pre, rank_in)


def expert_forward(arrived, tables, w_gate_up, w_down):
    gate_pre, up_pre, rank_in = expert_hidden(arrived, tables, w_gate_up, w_down.shape[1])
    activated = (jax.nn.silu(gate_pre) * up_pre).astype(jnp.bfloat16)
    rank_mid = bdot("jecf,jefr->jecr", activated, tables[2]).astype(jnp.bfloat16)
    result = bdot("jecf,efd->jecd", activated, w_down) + ADAPT_SCALE * bdot(
        "jecr,jerd->jecd", rank_mid, tables[3]
    )
    return result.astype(jnp.bfloat16)


def expert_backward(arrived, d_result, tables, w_gate_up, w_down):
    gate_pre, up_pre, rank_in = expert_hidden(arrived, tables, w_gate_up, w_down.shape[1])
    rank_dim = tables[1].shape[3]
    sigmoid_gate = jax.nn.sigmoid(gate_pre)
    silu_gate = gate_pre * sigmoid_gate
    activated = (silu_gate * up_pre).astype(jnp.bfloat16)
    rank_mid = bdot("jecf,jefr->jecr", activated, tables[2]).astype(jnp.bfloat16)
    d_rank_mid = (ADAPT_SCALE * bdot("jecd,jerd->jecr", d_result, tables[3])).astype(jnp.bfloat16)
    grad_out_up = ADAPT_SCALE * bdot("jecr,jecd->jerd", rank_mid, d_result)
    grad_out_down = bdot("jecf,jecr->jefr", activated, d_rank_mid)
    d_act = (
        (bdot("jecd,efd->jecf", d_result, w_down) + bdot("jecr,jefr->jecf", d_rank_mid, tables[2]))
        .astype(jnp.bfloat16)
        .astype(jnp.float32)
    )
    d_gate = (d_act * up_pre * sigmoid_gate * (1.0 + gate_pre * (1.0 - sigmoid_gate))).astype(
        jnp.bfloat16
    )
    d_up = (d_act * silu_gate).astype(jnp.bfloat16)
    d_rank_in = (
        ADAPT_SCALE
        * jnp.concatenate(
            [
                bdot("jecf,jerf->jecr", d_gate, tables[1][:, :, 0]),
                bdot("jecf,jerf->jecr", d_up, tables[1][:, :, 1]),
            ],
            -1,
        )
    ).astype(jnp.bfloat16)
    grad_in_up = ADAPT_SCALE * jnp.stack(
        [
            bdot("jecr,jecf->jerf", rank_in[..., :rank_dim], d_gate),
            bdot("jecr,jecf->jerf", rank_in[..., rank_dim:], d_up),
        ],
        2,
    )
    grad_in_down = bdot("jecd,jecr->jedr", arrived, d_rank_in)
    d_arrived = bdot("jecf,edf->jecd", jnp.concatenate([d_gate, d_up], -1), w_gate_up) + bdot(
        "jecr,jedr->jecd", d_rank_in, tables[0]
    )
    return (d_arrived, (grad_in_down, grad_in_up, grad_out_down, grad_out_up))


def local(
    hidden_in,
    prev_logits,
    segment_ids,
    routes,
    adapter_ids,
    attn_gain,
    w_qkv,
    w_out,
    attn_down,
    attn_up,
    ffn_gain,
    router_weight,
    gate_mix,
    const_mix,
    const_vec,
    w_gate_up,
    w_down,
    exp_in_down,
    exp_in_up,
    exp_out_down,
    exp_out_up,
    cotangent,
):
    tok_count = hidden_in.shape[1]
    model_dim = hidden_in.shape[2]
    kind_count = prev_logits.shape[2]
    local_experts = w_gate_up.shape[0]
    adapter_count = attn_down.shape[0]
    key_block = min(512, tok_count)
    ctx_size = lax.axis_size("context")
    ctx_index = lax.axis_index("context")
    exp_size = lax.axis_size("expert")
    exp_index = lax.axis_index("expert")
    dp_index = lax.axis_index("dp")
    ffn_count = local_experts * exp_size
    capacity = tok_count // 4
    seq_total = tok_count * ctx_size
    my_adapter = lax.dynamic_index_in_dim(
        adapter_ids, dp_index * exp_size + exp_index, 0, keepdims=False
    )
    tok_pos = ctx_index * tok_count + jnp.arange(tok_count, dtype=jnp.int32)
    rope_pos = tok_pos.astype(jnp.float32)
    seg_local = segment_ids[0]
    head_shape = (tok_count, HEADS, model_dim // HEADS)
    resid_in = hidden_in[0].astype(jnp.float32)
    gain_one = attn_gain.astype(jnp.float32)
    inv_one = lax.rsqrt(jnp.mean(resid_in * resid_in, -1, keepdims=True) + EPSILON)
    normed_low = (resid_in * inv_one * gain_one).astype(jnp.bfloat16)
    down_sel = lax.dynamic_index_in_dim(attn_down, my_adapter, 0, keepdims=False)
    up_sel = lax.dynamic_index_in_dim(attn_up, my_adapter, 0, keepdims=False)
    rank_qkv = bdot("td,pdr->ptr", normed_low, down_sel[:3]).astype(jnp.bfloat16)
    proj_qkv = bdot("td,de->te", normed_low, w_qkv).reshape(
        tok_count, 3, model_dim
    ) + ADAPT_SCALE * bdot("ptr,prd->tpd", rank_qkv, up_sel[:3])
    queries = rotate(proj_qkv[:, 0].reshape(head_shape), rope_pos, 1.0).astype(jnp.bfloat16)
    key_rows = rotate(proj_qkv[:, 1].reshape(head_shape), rope_pos, 1.0).astype(jnp.bfloat16)
    value_rows = proj_qkv[:, 2].reshape(head_shape).astype(jnp.bfloat16)
    all_keys, all_values, all_segs = (
        lax.all_gather(key_rows, "context", axis=0, tiled=True),
        lax.all_gather(value_rows, "context", axis=0, tiled=True),
        lax.all_gather(seg_local, "context", axis=0, tiled=True),
    )
    block_total = seq_total // key_block

    def key_slice(block_index):
        offset = block_index * key_block
        return (
            lax.dynamic_slice_in_dim(all_keys, offset, key_block, 0),
            lax.dynamic_slice_in_dim(all_values, offset, key_block, 0),
            lax.dynamic_slice_in_dim(all_segs, offset, key_block, 0),
            offset + jnp.arange(key_block, dtype=jnp.int32),
        )

    def max_step(block_index, totals):
        run_max, run_sum = totals
        blk_keys, blk_values, blk_segs, blk_pos = key_slice(block_index)
        scores = masked_scores(queries, blk_keys, tok_pos, seg_local, blk_pos, blk_segs)
        new_max = jnp.maximum(run_max, jnp.max(scores, -1))
        new_sum = run_sum * jnp.exp(run_max - new_max) + jnp.sum(
            jnp.exp(scores - new_max[:, :, None]), -1
        )
        return (new_max, new_sum)

    start_max = jnp.full((HEADS, tok_count), NEG, jnp.float32)
    run_max, run_sum = lax.fori_loop(
        0, block_total, max_step, (start_max, jnp.zeros((HEADS, tok_count), jnp.float32))
    )
    log_total = run_max + jnp.log(run_sum)

    def value_step(block_index, totals):
        high_acc, low_acc = totals
        blk_keys, blk_values, blk_segs, blk_pos = key_slice(block_index)
        probs_block = jnp.exp(
            masked_scores(queries, blk_keys, tok_pos, seg_local, blk_pos, blk_segs)
            - log_total[:, :, None]
        )
        rounded = probs_block.astype(jnp.bfloat16)
        residue = (probs_block - rounded.astype(jnp.float32)).astype(jnp.bfloat16)
        return (
            high_acc + bdot("hqk,khd->qhd", rounded, blk_values),
            low_acc + bdot("hqk,khd->qhd", residue, blk_values),
        )

    zero_heads = jnp.zeros(head_shape, jnp.float32)
    attn_high, attn_low = lax.fori_loop(0, block_total, value_step, (zero_heads, zero_heads))
    attn_exact = attn_high + attn_low
    attn_flat = attn_high.reshape(tok_count, model_dim).astype(jnp.bfloat16)
    rank_out = bdot("td,dr->tr", attn_flat, down_sel[3]).astype(jnp.bfloat16)
    mid_resid = (
        resid_in
        + bdot("td,de->te", attn_flat, w_out)
        + ADAPT_SCALE * bdot("tr,rd->td", rank_out, up_sel[3])
    )
    gain_two = ffn_gain.astype(jnp.float32)
    inv_two = lax.rsqrt(jnp.mean(mid_resid * mid_resid, -1, keepdims=True) + EPSILON)
    normed_two = mid_resid * inv_two * gain_two
    rows_low = normed_two.astype(jnp.bfloat16)
    logits = bdot("td,de->te", rows_low, router_weight) + fdot(
        "te,ef->tf", prev_logits[0], gate_mix
    )
    probs_all = jax.nn.softmax(logits, -1)
    route_tok = routes[0]
    kind_match = (
        route_tok[:, :, None] == jnp.arange(kind_count, dtype=jnp.int32)[None, None, :]
    ).astype(jnp.float32)
    gate_values = jnp.sum(kind_match * probs_all[:, None, :], -1)
    mix_const = jax.nn.softmax(bdot("td,idc->tic", rows_low, const_mix), -1)
    const_full = const_vec.astype(jnp.float32)
    const_terms = (
        mix_const[:, :, 0:1] * normed_two[:, None, :]
        + mix_const[:, :, 1:2] * const_full[None, :, :]
    )
    flat_route = route_tok.reshape(-1)
    is_ffn = flat_route < ffn_count
    ffn_match = (flat_route[:, None] == jnp.arange(ffn_count, dtype=jnp.int32)[None, :]).astype(
        jnp.int32
    )
    slot_rank = jnp.sum((jnp.cumsum(ffn_match, 0) - 1) * ffn_match, 1)
    slot_index = jnp.where(is_ffn, flat_route * capacity + slot_rank, ffn_count * capacity)
    safe_index = jnp.minimum(slot_index, ffn_count * capacity - 1)
    buffer_shape = (exp_size, local_experts, capacity, model_dim)
    outgoing = (
        jnp.zeros((ffn_count * capacity, model_dim), jnp.bfloat16)
        .at[slot_index]
        .set(jnp.repeat(rows_low, 2, 0), mode="drop")
        .reshape(buffer_shape)
    )
    source_ids = lax.dynamic_slice_in_dim(adapter_ids, dp_index * exp_size, exp_size, 0)
    source_match = source_ids[:, None] == jnp.arange(adapter_count, dtype=jnp.int32)[None, :]
    pick_table = source_match.astype(jnp.bfloat16)
    tables = tuple(
        (
            bdot("ja,a...->j...", pick_table, table_in).astype(jnp.bfloat16)
            for table_in in (exp_in_down, exp_in_up, exp_out_down, exp_out_up)
        )
    )
    arrived = lax.all_to_all(outgoing, "expert", split_axis=0, concat_axis=0, tiled=True)
    result = expert_forward(arrived, tables, w_gate_up, w_down)
    returned = lax.all_to_all(result, "expert", split_axis=0, concat_axis=0, tiled=True)
    ffn_rows = jnp.where(
        is_ffn[:, None], returned.reshape(ffn_count * capacity, model_dim)[safe_index], 0.0
    ).reshape(tok_count, 2, model_dim)
    branch_terms = ffn_rows.astype(jnp.float32) + jnp.where(
        (route_tok == ffn_count + 1)[:, :, None], normed_two[:, None, :], 0.0
    )
    for const_index in range(2):
        branch_terms = branch_terms + jnp.where(
            (route_tok == ffn_count + 2 + const_index)[:, :, None],
            const_terms[:, const_index][:, None, :],
            0.0,
        )
    layer_out = mid_resid + jnp.sum(gate_values[:, :, None] * branch_terms, 1)
    d_out = cotangent[0].astype(jnp.float32)
    d_gates = jnp.sum(d_out[:, None, :] * branch_terms, -1)
    d_kinds = jnp.sum(kind_match * d_gates[:, :, None], 1)
    d_logits = probs_all * (d_kinds - jnp.sum(probs_all * d_kinds, -1, keepdims=True))
    grad_prev = fdot("tf,ef->te", d_logits, gate_mix)
    d_normed = fdot("te,de->td", d_logits, router_weight.astype(jnp.float32))
    copy_weight = jnp.sum(gate_values * (route_tok == ffn_count + 1).astype(jnp.float32), 1)
    d_normed = d_normed + copy_weight[:, None] * d_out
    for const_index in range(2):
        const_weight = jnp.sum(
            gate_values * (route_tok == ffn_count + 2 + const_index).astype(jnp.float32), 1
        )
        d_term = const_weight[:, None] * d_out
        mix_pair = mix_const[:, const_index]
        d_normed = d_normed + mix_pair[:, 0:1] * d_term
        d_mix = jnp.stack(
            [
                jnp.sum(d_term * normed_two, -1),
                jnp.sum(d_term * const_full[const_index][None, :], -1),
            ],
            -1,
        )
        d_inner = mix_pair * (d_mix - jnp.sum(mix_pair * d_mix, -1, keepdims=True))
        d_normed = d_normed + fdot("tc,dc->td", d_inner, const_mix[const_index].astype(jnp.float32))
    d_pairs = (
        (gate_values[:, :, None] * d_out[:, None, :])
        .astype(jnp.bfloat16)
        .reshape(2 * tok_count, model_dim)
    )
    d_outgoing = (
        jnp.zeros((ffn_count * capacity, model_dim), jnp.bfloat16)
        .at[slot_index]
        .set(d_pairs, mode="drop")
        .reshape(buffer_shape)
    )
    d_arrived = lax.all_to_all(d_outgoing, "expert", split_axis=0, concat_axis=0, tiled=True)
    d_kept, owner_grads = expert_backward(arrived, d_arrived, tables, w_gate_up, w_down)
    d_back = lax.all_to_all(
        d_kept.astype(jnp.bfloat16), "expert", split_axis=0, concat_axis=0, tiled=True
    ).astype(d_kept.dtype)
    d_back_rows = jnp.where(
        is_ffn[:, None], d_back.reshape(ffn_count * capacity, model_dim)[safe_index], 0.0
    ).reshape(tok_count, 2, model_dim)
    d_normed = d_normed + jnp.sum(d_back_rows, 1)
    scaled_two = d_normed * gain_two
    d_mid = (
        d_out
        + inv_two * scaled_two
        - mid_resid
        * (inv_two * inv_two * inv_two)
        * jnp.mean(scaled_two * mid_resid, -1, keepdims=True)
    )
    d_branch = d_mid.astype(jnp.bfloat16)
    d_rank_out = (ADAPT_SCALE * bdot("td,rd->tr", d_branch, up_sel[3])).astype(jnp.bfloat16)
    grad_up_out = ADAPT_SCALE * bdot("tr,td->rd", rank_out, d_branch)
    grad_down_out = bdot("td,tr->dr", attn_flat, d_rank_out)
    d_attn = (
        (bdot("te,de->td", d_branch, w_out) + bdot("tr,dr->td", d_rank_out, down_sel[3]))
        .astype(jnp.bfloat16)
        .reshape(head_shape)
    )
    row_delta = jnp.transpose(jnp.sum(d_attn.astype(jnp.float32) * attn_exact, -1))

    def grad_step(block_index, totals):
        d_query_acc, d_key_all, d_value_all = totals
        blk_keys, blk_values, blk_segs, blk_pos = key_slice(block_index)
        d_query_part, d_key_part, d_value_part = block_grads(
            queries,
            d_attn,
            log_total,
            row_delta,
            tok_pos,
            seg_local,
            blk_keys,
            blk_values,
            blk_pos,
            blk_segs,
        )
        offset = block_index * key_block
        return (
            d_query_acc + d_query_part,
            lax.dynamic_update_slice_in_dim(d_key_all, d_key_part, offset, 0),
            lax.dynamic_update_slice_in_dim(d_value_all, d_value_part, offset, 0),
        )

    zero_all = jnp.zeros((seq_total,) + head_shape[1:], jnp.float32)
    d_queries, d_key_all, d_value_all = lax.fori_loop(
        0, block_total, grad_step, (zero_heads, zero_all, zero_all)
    )
    d_keys, d_values = (
        lax.psum_scatter(
            d_key_all.astype(jnp.bfloat16), "context", scatter_dimension=0, tiled=True
        ).astype(jnp.float32),
        lax.psum_scatter(
            d_value_all.astype(jnp.bfloat16), "context", scatter_dimension=0, tiled=True
        ).astype(jnp.float32),
    )
    d_query_flat = rotate(d_queries, rope_pos, -1.0).reshape(tok_count, model_dim)
    d_key_flat = rotate(d_keys, rope_pos, -1.0).reshape(tok_count, model_dim)
    d_proj = jnp.stack(
        [d_query_flat, d_key_flat, d_values.reshape(tok_count, model_dim)], 1
    ).astype(jnp.bfloat16)
    d_rank_qkv = (ADAPT_SCALE * bdot("tpd,prd->ptr", d_proj, up_sel[:3])).astype(jnp.bfloat16)
    grad_up_qkv = ADAPT_SCALE * bdot("ptr,tpd->prd", rank_qkv, d_proj)
    grad_down_qkv = bdot("td,ptr->pdr", normed_low, d_rank_qkv)
    d_normed_one = bdot("te,de->td", d_proj.reshape(tok_count, 3 * model_dim), w_qkv) + bdot(
        "ptr,pdr->td", d_rank_qkv, down_sel[:3]
    )
    scaled_one = d_normed_one * gain_one
    grad_in = (
        d_mid
        + inv_one * scaled_one
        - resid_in
        * (inv_one * inv_one * inv_one)
        * jnp.mean(scaled_one * resid_in, -1, keepdims=True)
    )
    own_match = (jnp.arange(adapter_count, dtype=jnp.int32) == my_adapter).astype(jnp.float32)
    down_table = (
        own_match[:, None, None, None]
        * jnp.concatenate([grad_down_qkv, grad_down_out[None]], 0)[None]
    )
    up_table = (
        own_match[:, None, None, None] * jnp.concatenate([grad_up_qkv, grad_up_out[None]], 0)[None]
    )
    grad_attn_down, grad_attn_up = lax.psum((down_table, up_table), ("dp", "context", "expert"))
    source_full = source_match.astype(jnp.float32)
    part_in_down = fdot("ja,j...->a...", source_full, owner_grads[0])
    part_in_up = fdot("ja,j...->a...", source_full, owner_grads[1])
    part_out_down = fdot("ja,j...->a...", source_full, owner_grads[2])
    part_out_up = fdot("ja,j...->a...", source_full, owner_grads[3])
    grad_in_down, grad_in_up, grad_out_down, grad_out_up = lax.psum(
        (part_in_down, part_in_up, part_out_down, part_out_up), ("dp", "context")
    )
    return (
        layer_out.astype(jnp.bfloat16)[None],
        grad_in[None],
        grad_prev[None],
        grad_attn_down,
        grad_attn_up,
        grad_in_down,
        grad_in_up,
        grad_out_down,
        grad_out_up,
    )


def solution(mesh):
    return jax.shard_map(
        local,
        mesh=mesh,
        in_specs=(
            P(("dp", "expert"), "context", None),
            P(("dp", "expert"), "context", None),
            P(("dp", "expert"), "context"),
            P(("dp", "expert"), "context", None),
            P(),
            P(),
            P(),
            P(),
            P(),
            P(),
            P(),
            P(),
            P(),
            P(),
            P(),
            P("expert", None, None),
            P("expert", None, None),
            P(None, "expert", None, None),
            P(None, "expert", None, None, None),
            P(None, "expert", None, None),
            P(None, "expert", None, None),
            P(("dp", "expert"), "context", None),
        ),
        out_specs=(
            P(("dp", "expert"), "context", None),
            P(("dp", "expert"), "context", None),
            P(("dp", "expert"), "context", None),
            P(),
            P(),
            P(None, "expert", None, None),
            P(None, "expert", None, None, None),
            P(None, "expert", None, None),
            P(None, "expert", None, None),
        ),
        check_vma=False,
    )
```

profile of v0, /device:TPU:25, one launch (start us, length us, event | category | flops | bytes accessed | tf_op | source)
XLA Modules:
  0.0 991.0 jit_solution(347246996769072440)
XLA Ops:
  12.7 5.8 copy.234
  70.7 5.3 mul.790
  76.1 30.8 %while.50 = (s32[]{:T(128)}, f32[12,512]{1,0:T(8,128)S(1)}, f32[12,512]{1,0:T(8,128)S(1)}, s32[1,512]{1,0:T(1,128)S(1)}, s32[1024]{0:T(1024)S(1)}, /*index=5*/bf...) while((s32[]{:T(128)}, f32[12,512]{1,0:T(8,128)S(1)}, ...), condition=%wide.region_4.5_spmd.clone, body=%wide.region_1.4_spmd.clone.sunk | while | flops 425491456 | bytes 27861180 | solution.py:227
  76.7 7.8 fusion.327
  84.4 7.1 exponential_reduce_fusion.2
  92.0 7.7 fusion.327
  99.7 7.1 exponential_reduce_fusion.2
  107.0 45.0 %while.51 = (s32[]{:T(128)}, f32[512,12,64]{0,2,1:T(8,128)}, f32[512,12,64]{0,2,1:T(8,128)}, bf16[1024,12,64]{0,2,1:T(8,128)(2,1)}, s32[1,512]{1,0:T(1,128)S(1)}...) while((s32[]{:T(128)}, f32[512,12,64]{0,2,1:T(8,128)}, ...), condition=%wide.region_6.7_spmd.clone, body=%wide.region_5.6_spmd.clone.sunk | while | flops 1244922880 | bytes 104669448 | solution.py:247
  107.4 7.5 fusion.334
  114.9 9.7 bitcast_add_fusion.12
  129.0 7.5 fusion.334
  136.6 10.1 %bitcast_add_fusion.12 = f32[512,12,64]{0,2,1:T(8,128)} fusion(f32[512,12,64]{0,2,1:T(8,128)} %get-tuple-element.1107, f32[12,512,512]{2,1,0:T(8,128)} %fusion.334, f32[12,512]{1,0:T(8,128)S(1)} %get-tuple-element.1127, pred[512,512]{0,1:T(8,128)(4,1)S(1)} %compare_and_fusion.7, pred[]{:T(512)S(6)} %compare.10, ...), kind=kOutput, calls=%fused_computation.31.clone.1 | convolution fusion | flops 425459712 | bytes 16801796 | tf_op jit(solution)/shard_map/while/body/eval_jaxpr/hqk,khd->qhd/dot_general | solution.py:37
  146.7 5.2 bitcast_add_fusion.11
  165.1 7.0 scatter_custom_fusion
  172.2 6.8 all-to-all-start
  187.9 10.3 %all-to-all-done = bf16[4,2,128,768]{3,2,1,0:T(8,128)(2,1)} async-done(((bf16[4,2,128,768]{3,2,1,0:T(8,128)(2,1)}), bf16[4,2,128,768]{3,2,1,0:T(8,128)(2,1)}, u32[]{:S(2)}, u32[]{:S(2)}) %all-to-all-start) | async-done | bytes 1572896 | tf_op jit(solution)/shard_map/all_to_all | solution.py:299
  200.3 15.1 %fusion.58 = f32[4,2,128,4096]{3,2,0,1:T(8,128)} fusion(bf16[2,768,4096]{2,1,0:T(8,128)(2,1)} %param.43, bf16[4,2,128,768]{3,2,1,0:T(8,128)(2,1)} %all-to-all-done), kind=kOutput, calls=%fused_computation.77 | convolution fusion | flops 6442450944 | bytes 30932992 | tf_op jit(solution)/shard_map/jecd,edf->jecf/dot_general | solution.py:37
  215.3 4.9 slice_add_fusion.1
  220.3 10.5 %multiply_convert_fusion = (bf16[4,2,128,2048]{3,2,0,1:T(8,128)(2,1)S(1)}, f32[4,2,128,2048]{3,2,0,1:T(8,128)}) fusion(f32[4,2,128,2048]{3,2,0,1:T(8,128)S(1)} %slice_add_fusion.1, bf16[4,2,16,2048]{3,0,2,1:T(4,128)(2,1)S(1)} %copy-done.51, bf16[4,2,128,16]{2,3,1,0:T(8,128)(2,1)S(1)} %get-tuple-element.818, f32[4,2,128,4096]{3,2,0,1:T(8,128)} %fusion.58), kind=kOutput, calls=%fused_computation.89 | convolution fusion | flops 83886080 | bytes 29917184 | tf_op jit(solution)/shard_map/jecr,jerf->jecf/dot_general | solution.py:37
  237.7 5.4 all-to-all-start.1
  250.1 5.3 broadcast_in_dim.327
  259.6 5.3 broadcast_in_dim.330
  269.0 5.3 broadcast_in_dim.323
  275.0 7.2 gather_fusion
  282.2 5.9 multiply_reduce_fusion
  288.9 7.6 scatter_custom_fusion.1
  301.3 19.2 %all-to-all-done.2 = bf16[4,2,128,768]{3,2,1,0:T(8,128)(2,1)} async-done(((bf16[4,2,128,768]{3,2,1,0:T(8,128)(2,1)}), bf16[4,2,128,768]{3,2,1,0:T(8,128)(2,1)}, u32[]{:S(2)}, u32[]{:S(2)}) %all-to-all-start.2) | async-done | bytes 1572896 | tf_op jit(solution)/shard_map/all_to_all | solution.py:350
  320.5 10.0 %fusion.70 = f32[2,4,128,2048]{3,2,1,0:T(8,128)} fusion(bf16[2,2048,768]{2,1,0:T(8,128)(2,1)} %param.44, bf16[4,2,128,768]{3,2,1,0:T(8,128)(2,1)} %all-to-all-done.2), kind=kOutput, calls=%fused_computation.92 | convolution fusion | flops 3221225472 | bytes 16252928 | tf_op jit(solution)/shard_map/jecd,efd->jecf/dot_general | solution.py:37
  332.6 10.6 %fusion.63 = (bf16[4,2,128,2048]{3,2,0,1:T(8,128)(2,1)S(1)}, bf16[4,2,128,2048]{3,2,0,1:T(8,128)(2,1)S(1)}) fusion(f32[4,2,128,2048]{3,2,0,1:T(8,128)} %get-tuple-element.841, f32[4,2,128,2048]{3,2,0,1:T(8,128)} %copy-done.17, bf16[4,2,2048,16]{2,0,3,1:T(4,128)(2,1)S(1)} %copy-done.50, bf16[4,2,128,16]{2,3,1,0:T(8,128)(2,1)S(1)} %fusion.142, ...), kind=kOutput, calls=%fused_computation.80 | convolution fusion | flops 100663296 | bytes 34111488 | tf_op jit(solution)/shard_map/jecr,jefr->jecf/dot_general | solution.py:37
  349.0 14.1 %fusion.86 = bf16[4,2,128,768]{3,2,0,1:T(8,128)(2,1)} fusion(f32[4,2,128,768]{3,2,0,1:T(8,128)} %fusion.173, bf16[2,768,4096]{2,1,0:T(8,128)(2,1)} %param.43, bf16[4,2,128,2048]{3,2,0,1:T(8,128)(2,1)} %copy-done.24, bf16[4,2,128,2048]{3,2,0,1:T(8,128)(2,1)} %copy-done.26), kind=kOutput, calls=%fused_computation.111 | convolution fusion | flops 6460801024 | bytes 25690112 | tf_op jit(solution)/shard_map/jecf,edf->jecd/dot_general | solution.py:37
  365.9 5.2 all-to-all-start.3
  382.6 7.8 all-to-all-done.3
  393.8 7.8 gather_fusion.1
  401.6 5.2 gather.13
  406.8 14.6 %select_reduce_fusion = (f32[512,768]{1,0:T(8,128)S(1)}, f32[512,768]{1,0:T(8,128)S(1)}) fusion(f32[512,2,768]{2,1,0:T(2,128)} %gather.13, pred[512,2]{1,0:T(8,128)(4,1)S(1)} %copy-done.47, f32[512,768]{1,0:T(8,128)} %get-tuple-element.848, pred[512,2]{1,0:T(8,128)(4,1)S(1)} %copy-done.45, f32[512,768]{1,0:T(8,128)} %copy-done.12, ...), kind=kLoop, calls=%fused_computation.114 | loop fusion | flops 8650752 | bytes 12591104 | tf_op jit(solution)/shard_map/reduce_sum | solution.py:358
  433.3 66.7 %while.52 = (s32[]{:T(128)}, f32[512,12,64]{0,2,1:T(8,128)}, bf16[1024,12,64]{0,2,1:T(8,128)(2,1)}, bf16[1024,12,64]{0,2,1:T(8,128)(2,1)}, bf16[1024,12,64]{0,2,...) while((s32[]{:T(128)}, f32[512,12,64]{0,2,1:T(8,128)}, ...), condition=%wide.region_35.36_spmd.clone, body=%wide.region_34.35_spmd.clone.sunk | while | flops 2047083520 | bytes 100770080 | solution.py:401
  433.8 7.7 fusion.345
  441.5 7.0 fusion.346
  454.0 5.3 bitcast_add_fusion.13
  459.3 7.2 bitcast_dynamic-update-slice_fusion.5
  466.9 7.7 fusion.345
  474.6 7.0 fusion.346
  487.1 5.7 bitcast_add_fusion.13
  492.8 7.2 bitcast_dynamic-update-slice_fusion.5
  529.1 26.2 %reduce-scatter.5.cloned.1.call-done = bf16[512,12,64]{0,2,1:T(8,128)(2,1)} async-done(((bf16[1024,12,64]{0,2,1:T(8,128)(2,1)}), bf16[512,12,64]{0,2,1:T(8,128)(2,1)}) %reduce-scatter.5.cloned.1.call-update) | async-done | bytes 786448 | tf_op jit(solution)/shard_map/reduce_scatter | solution.py:408
  576.9 260.4 %all-reduce.7.cloned.1.call-done = (f32[8,2,768,32]{2,0,3,1:T(8,128)}, f32[8,2,2,16,2048]{4,0,3,2,1:T(8,128)}, f32[8,2,2048,16]{2,0,3,1:T(8,128)}, f32[8,2,16,768]{3,0,2,1:T(8,128)}) async-done(((f32[8,2,768,32]{2,0,3,1:T(8,128)}, f32[8,2,2,16,2048]{4,0,3,2,1:T(8,128)}, f32[8,2,2048,16]{2,0,3,1:T(8,128)}, f32[8,2,16,768]{3,0,2,1:T(8,128)}), (f32[8,2,768,32]{2,0,3,1:T(8,128)}, ...) | async-done | bytes 8650768 | tf_op jit(solution)/shard_map/psum | solution.py:445
  837.3 6.8 copy.296
  849.4 130.7 %all-reduce.5.cloned.1.call-done = (f32[8,4,768,16]{2,3,1,0:T(8,128)}, f32[8,4,16,768]{3,2,1,0:T(8,128)}) async-done(((f32[8,4,768,16]{2,3,1,0:T(8,128)}, f32[8,4,16,768]{3,2,1,0:T(8,128)}), (f32[8,4,768,16]{2,3,1,0:T(8,128)}, f32[8,4,16,768]{3,2,1,0:T(8,128)})) %all-reduce.5.cloned.1.call-update) | async-done | bytes 3145744 | tf_op jit(solution)/shard_map/psum | solution.py:439
  (427 shorter events, 221.7 us)
Async XLA Ops:
  7.2 50.5 %copy-start = (bf16[8,2,2,16,2048]{4,3,2,1,0:T(8,128)(2,1)S(1)}, bf16[8,2,2,16,2048]{4,3,2,1,0:T(8,128)(2,1)}, u32[]{:S(2)}) copy-start(bf16[8,2,2,16,2048]{4,3,2,1,0:T(8,128)(2,1)} %param.46) | copy-start | bytes 6291460
  7.2 68.9 %all-gather.6.cloned.1.call-start = ((), (), s32[]{:S(2)}) async-start(), calls=%async_computation.7 | async-start | bytes 2359296 | tf_op jit(solution)/shard_map/all_gather | solution.py:201
  12.0 11.3 %copy-start.91 = (f32[512]{0:T(512)}, f32[512]{0:T(512)S(1)}, u32[]{:S(2)}) copy-start(f32[512]{0:T(512)S(1)} %get-tuple-element.833) | copy-start | bytes 6148
  12.7 10.6 %copy-start.88 = (f32[768]{0:T(1024)}, f32[768]{0:T(1024)S(1)}, u32[]{:S(2)}) copy-start(f32[768]{0:T(1024)S(1)} %convert_element_type.235) | copy-start | bytes 9220
  12.7 6.5 copy-start.13
  41.3 65.6 %all-gather.4.cloned.1.call-start = ((), (), s32[]{:S(2)}) async-start(), calls=%async_computation.6 | async-start | bytes 2359296 | tf_op jit(solution)/shard_map/all_gather | solution.py:202
  43.7 7.8 copy-start.100
  46.1 9.0 copy-start.103
  47.9 16.0 %copy-start.81 = (pred[512,2]{0,1:T(4,128)(4,1)}, pred[512,2]{0,1:T(4,128)(4,1)S(1)}, u32[]{:S(2)}) copy-start(pred[512,2]{0,1:T(4,128)(4,1)S(1)} %get-tuple-element.826) | copy-start | bytes 3076
  55.1 7.0 copy-start.78
  60.5 6.3 copy-start.93
  60.5 7.3 copy-start.15
  63.3 101.9 %copy-start.98 = (s32[1024,1]{0,1:T(1,128)}, s32[1024,1]{0,1:T(1,128)S(1)}, u32[]{:S(2)}) copy-start(s32[1024,1]{0,1:T(1,128)S(1)} %get-tuple-element.820) | copy-start | bytes 12292
  70.7 5.4 copy-start.33
  114.9 9.7 copy-start.3
  114.9 9.7 copy-start.101
  136.6 10.1 %copy-start.3 = (f32[12,512,512]{2,1,0:T(8,128)S(1)}, f32[12,512,512]{2,1,0:T(8,128)}, u32[]{:S(2)}) copy-start(f32[12,512,512]{2,1,0:T(8,128)} %fusion.334) | copy-start | bytes 37748740 | tf_op jit(solution)/shard_map/while
  136.6 10.1 %copy-start.101 = (bf16[1024,12,64]{0,2,1:T(8,128)(2,1)S(1)}, bf16[1024,12,64]{0,2,1:T(8,128)(2,1)}, u32[]{:S(2)}) copy-start(bf16[1024,12,64]{0,2,1:T(8,128)(2,1)} %get-tuple-element.1122) | copy-start | bytes 4718596 | tf_op jit(solution)/shard_map/while
  172.2 6.8 copy-start.80
  172.2 26.0 %all-to-all-start = ((bf16[4,2,128,768]{3,2,1,0:T(8,128)(2,1)}), bf16[4,2,128,768]{3,2,1,0:T(8,128)(2,1)}, u32[]{:S(2)}, u32[]{:S(2)}) async-start(bf16[4,2,128,768]{3,2,1,0:T(8,128)(2,1)} %bitcast.380), calls=%async_computation | async-start | bytes 3145728 | tf_op jit(solution)/shard_map/all_to_all | solution.py:299
  183.7 14.5 %copy-start.31 = (bf16[4,2,768,32]{2,0,3,1:T(4,128)(2,1)S(1)}, bf16[4,2,768,32]{2,0,3,1:T(4,128)(2,1)}, u32[]{:S(2)}) copy-start(bf16[4,2,768,32]{2,0,3,1:T(4,128)(2,1)} %convolution_convert_fusion.2) | copy-start | bytes 1179652
  200.2 15.1 %copy-start.59 = (bf16[4,2,128,32]{2,3,1,0:T(8,128)(2,1)}, bf16[4,2,128,32]{2,3,1,0:T(8,128)(2,1)S(1)}, u32[]{:S(2)}) copy-start(bf16[4,2,128,32]{2,3,1,0:T(8,128)(2,1)S(1)} %convolution_convert_fusion.4) | copy-start | bytes 196612
  215.3 17.5 %slice-start = ((s8[6291456]{0:T(1024)(128)(4,1)}), s8[4194304]{0:T(1024)(128)(4,1)S(1)}, s32[]{:S(2)}) async-start(s8[6291456]{0:T(1024)(128)(4,1)} %bitcast.415), calls=%async_computation.12 | async-start | bytes 8388608
  220.2 10.5 %copy-start.17 = (f32[4,2,128,2048]{3,2,0,1:T(8,128)}, f32[4,2,128,2048]{3,2,0,1:T(8,128)S(1)}, u32[]{:S(2)}) copy-start(f32[4,2,128,2048]{3,2,0,1:T(8,128)S(1)} %slice_add_fusion.1) | copy-start | bytes 25165828
  220.3 10.5 %copy-start.49 = (bf16[4,2,2048,16]{2,0,3,1:T(4,128)(2,1)S(1)}, bf16[4,2,2048,16]{2,0,3,1:T(4,128)(2,1)}, u32[]{:S(2)}) copy-start(bf16[4,2,2048,16]{2,0,3,1:T(4,128)(2,1)} %convolution_convert_fusion.1) | copy-start | bytes 1572868
  220.3 12.6 %slice-start.1 = ((s8[6291456]{0:T(1024)(128)(4,1)}), s8[2097152]{0:T(1024)(128)(4,1)S(1)}, s32[]{:S(2)}) async-start(s8[6291456]{0:T(1024)(128)(4,1)} %bitcast.415), calls=%async_computation.13 | async-start | bytes 4194304
  237.7 37.3 %all-to-all-start.1 = ((bf16[4,2,128,768]{3,2,1,0:T(8,128)(2,1)}), bf16[4,2,128,768]{3,2,1,0:T(8,128)(2,1)}, u32[]{:S(2)}, u32[]{:S(2)}) async-start(bf16[4,2,128,768]{3,2,1,0:T(8,128)(2,1)} %copy.259), calls=%async_computation.1 | async-start | bytes 3145728 | tf_op jit(solution)/shard_map/all_to_all | solution.py:301
  269.0 5.6 copy-start.72
  269.0 5.6 copy-start.76
  269.0 6.0 copy-start.73
  275.0 7.3 copy-start.94
  275.0 7.2 copy-start.95
  275.0 7.2 copy-start.96
  275.0 7.2 copy-start.97
  282.2 6.2 copy-start.70
  296.5 24.1 %all-to-all-start.2 = ((bf16[4,2,128,768]{3,2,1,0:T(8,128)(2,1)}), bf16[4,2,128,768]{3,2,1,0:T(8,128)(2,1)}, u32[]{:S(2)}, u32[]{:S(2)}) async-start(bf16[4,2,128,768]{3,2,1,0:T(8,128)(2,1)} %bitcast.383), calls=%async_computation.2 | async-start | bytes 3145728 | tf_op jit(solution)/shard_map/all_to_all | solution.py:350
  332.6 10.7 %copy-start.67 = (bf16[4,2,128,16]{2,3,1,0:T(8,128)(2,1)}, bf16[4,2,128,16]{2,3,1,0:T(8,128)(2,1)S(1)}, u32[]{:S(2)}) copy-start(bf16[4,2,128,16]{2,3,1,0:T(8,128)(2,1)S(1)} %fusion.142) | copy-start | bytes 98308
  365.9 24.6 %all-to-all-start.3 = ((bf16[4,2,128,768]{3,2,1,0:T(8,128)(2,1)}), bf16[4,2,128,768]{3,2,1,0:T(8,128)(2,1)}, u32[]{:S(2)}, u32[]{:S(2)}) async-start(bf16[4,2,128,768]{3,2,1,0:T(8,128)(2,1)} %copy.281), calls=%async_computation.3 | async-start | bytes 3145728 | tf_op jit(solution)/shard_map/all_to_all | solution.py:352
  371.1 155.4 %reduce-scatter.3.cloned.1.call-start = ((), (), s32[]{:S(2)}) async-start(), calls=%async_computation.8 | async-start | bytes 2359296 | tf_op jit(solution)/shard_map/reduce_scatter | solution.py:405
  406.8 14.6 %copy-start.10 = (f32[512,768]{1,0:T(8,128)S(1)}, f32[512,768]{1,0:T(8,128)}, u32[]{:S(2)}) copy-start(f32[512,768]{1,0:T(8,128)} %copy-done.9) | copy-start | bytes 4718596
  406.8 14.6 %copy-start.20 = (f32[512,768]{1,0:T(8,128)S(1)}, f32[512,768]{1,0:T(8,128)}, u32[]{:S(2)}) copy-start(f32[512,768]{1,0:T(8,128)} %fusion.200) | copy-start | bytes 4718596
  406.8 14.6 %copy-start.21 = (f32[512,768]{1,0:T(8,128)S(1)}, f32[512,768]{1,0:T(8,128)}, u32[]{:S(2)}) copy-start(f32[512,768]{1,0:T(8,128)} %fusion.207) | copy-start | bytes 4718596
  433.8 7.7 copy-start.102
  466.9 7.7 copy-start.102
  500.0 55.3 %reduce-scatter.5.cloned.1.call-start = ((), (), s32[]{:S(2)}) async-start(), calls=%async_computation.9 | async-start | bytes 2359296 | tf_op jit(solution)/shard_map/reduce_scatter | solution.py:408
  500.6 336.7 %all-reduce.7.cloned.1.call-start = ((), (), s32[]{:S(2)}) async-start(), calls=%async_computation.11 | async-start | bytes 17301504 | tf_op jit(solution)/shard_map/psum | solution.py:445
  523.1 456.9 %all-reduce.5.cloned.1.call-start = ((), (), s32[]{:S(2)}) async-start(), calls=%async_computation.10 | async-start | bytes 6291456 | tf_op jit(solution)/shard_map/psum | solution.py:439
  837.3 6.8 copy-start.27
  (72 other events, 193.9 us)
Sparse Core Ops, SparseCore 0:
  41.4 28.2 all-gather.5
  71.8 27.1 all-gather.3
  500.1 26.2 reduce-scatter.2
  529.2 26.0 reduce-scatter.4
  560.3 276.9 all-reduce.6
  844.3 135.6 all-reduce.4
where the time goes:
time: 1000 us; the launch traced here: 991 us
  waiting for transfers between devices  457 us (46%)
  matrix products  256 us (26%)
  local copies, waits for them, and re-layouts  153 us (15%)
  other arithmetic  80.5 us (8%)
  starting transfers between devices  22.9 us (2%)
  between operations  17.6 us (2%)
    psum x1, waiting for transfers between devices, local(): lax.psum((part_in_down, part_in_up, part_out_down, part_out_up), ('dp', '...  260 us
    dot_general x58, matrix products, bdot(): return jnp.einsum(form, left, right, preferred_element_type=jnp.float32)  237 us
    psum x1, waiting for transfers between devices, local(): lax.psum((down_table, up_table), ('dp', 'context', 'expert'))  131 us
    unnamed x214, local copies, waits for them, and re-layouts  34 us
    reduce_scatter x1, waiting for transfers between devices, local(): lax.psum_scatter(d_value_all.astype(jnp.bfloat16), 'context', scatter_dim...  26.2 us
  transfers between devices with their start and end apart: 10, of which 7 were waited for; matrix products, arithmetic and copies ran while one was open for 17% of the time, Pallas kernels for 0%

commit v1 on v0

--- a/solution.py
+++ b/solution.py
@@ -1,9 +1,17 @@
+import functools
 import math
 
 import jax
 import jax.numpy as jnp
 from jax import lax
+from jax.experimental import pallas as pl
+from jax.experimental.pallas import tpu as pltpu
 from jax.sharding import PartitionSpec as P
+
+MESH = pl.DeviceIdType.MESH
+VLIMIT = 60 * 1024 * 1024
+BF = jnp.bfloat16
+F32 = jnp.float32
 
 HEADS = 12
 
@@ -105,7 +113,7 @@
     rank_mid = bdot("jecf,jefr->jecr", activated, tables[2]).astype(jnp.bfloat16)
     d_rank_mid = (ADAPT_SCALE * bdot("jecd,jerd->jecr", d_result, tables[3])).astype(jnp.bfloat16)
     grad_out_up = ADAPT_SCALE * bdot("jecr,jecd->jerd", rank_mid, d_result)
-    grad_out_down = bdot("jecf,jecr->jefr", activated, d_rank_mid)
+    grad_out_down = bdot("jecf,jecr->jerf", activated, d_rank_mid)
     d_act = (
         (bdot("jecd,efd->jecf", d_result, w_down) + bdot("jecr,jefr->jecf", d_rank_mid, tables[2]))
         .astype(jnp.bfloat16)
@@ -132,11 +140,247 @@
         ],
         2,
     )
-    grad_in_down = bdot("jecd,jecr->jedr", arrived, d_rank_in)
+    grad_in_down = bdot("jecd,jecr->jerd", arrived, d_rank_in)
     d_arrived = bdot("jecf,edf->jecd", jnp.concatenate([d_gate, d_up], -1), w_gate_up) + bdot(
         "jecr,jedr->jecd", d_rank_in, tables[0]
     )
     return (d_arrived, (grad_in_down, grad_in_up, grad_out_down, grad_out_up))
+
+
+def to_tiles(table):
+    lead, (rows, cols) = table.shape[:-2], table.shape[-2:]
+    cut = table.reshape(lead + (rows // 16, 16, cols // 128, 128))
+    cut = jnp.swapaxes(cut, -3, -2)
+    return cut.reshape(lead + (rows * cols // 2048, 16, 128))
+
+
+def reduce_kernel(
+    sizes, ids_ref, grads_ref, attn_ref, table_ref, attn_table_ref,
+    held, arrived_x, part_z, arrived_z,
+    load_sem, ready_send, ready_recv, x_send, x_recv, z_send, z_recv, az_send, az_recv,
+    ax_send, ax_recv, e_send, e_recv,
+):
+    ctx_n, dp_n, exp_n, adapters, tiles, attn_tiles, x_tiles, z_tiles = sizes
+    own_attn = attn_tiles // exp_n
+    ctx, dp, exp = lax.axis_index("context"), lax.axis_index("dp"), lax.axis_index("expert")
+    barrier = pltpu.get_barrier_semaphore()
+    for axis, size, index in (("context", ctx_n, ctx), ("dp", dp_n, dp), ("expert", exp_n, exp)):
+        for step in range(1, size):
+            pl.semaphore_signal(
+                barrier, inc=1, device_id={axis: lax.rem(index + step, size)}, device_id_type=MESH
+            )
+    load = pltpu.make_async_copy(grads_ref, held.at[:, pl.ds(0, tiles)], load_sem)
+    load.start()
+    keep = pltpu.make_async_copy(
+        attn_ref.at[pl.ds(exp * own_attn, own_attn)],
+        held.at[exp, pl.ds(tiles, own_attn)],
+        ready_send.at[exp_n - 1],
+    )
+    keep.start()
+    pl.semaphore_wait(barrier, ctx_n + dp_n + exp_n - 3)
+
+    def copy(src, dst, send, recv, axis, target):
+        return pltpu.make_async_remote_copy(
+            src_ref=src, dst_ref=dst, send_sem=send, recv_sem=recv,
+            device_id={axis: target}, device_id_type=MESH,
+        )
+
+    waits = []
+    first = []
+    for step in range(1, exp_n):
+        peer = lax.rem(exp + step, exp_n)
+        send = copy(
+            attn_ref.at[pl.ds(peer * own_attn, own_attn)],
+            held.at[exp, pl.ds(tiles, own_attn)],
+            ready_send.at[step - 1], ready_recv.at[step - 1], "expert", peer,
+        )
+        send.start()
+        first.append(send)
+    load.wait()
+    keep.wait()
+    for send in first:
+        send.wait()
+    for k in range(1, dp_n + 1):
+        part = lax.rem(dp + k, dp_n)
+        for step in range(1, ctx_n):
+            peer = lax.rem(ctx + step, ctx_n)
+            send = copy(
+                held.at[:, pl.ds(peer * x_tiles + part * z_tiles, z_tiles)],
+                arrived_x.at[step - 1, k - 1],
+                x_send.at[step - 1, k - 1], x_recv.at[step - 1, k - 1], "context", peer,
+            )
+            send.start()
+            waits.append(send)
+    z_sends = []
+    for k in range(1, dp_n + 1):
+        part = lax.rem(dp + k, dp_n)
+        for step in range(1, ctx_n):
+            waits[(k - 1) * (ctx_n - 1) + step - 1].wait_recv()
+        base = ctx * x_tiles + part * z_tiles
+
+        def add(tile, carry, k=k, base=base):
+            total = held[:, pl.ds(base + tile, 1)].astype(F32)
+            for step in range(1, ctx_n):
+                total = total + arrived_x[step - 1, k - 1, :, pl.ds(tile, 1)].astype(F32)
+            part_z[k - 1, :, pl.ds(tile, 1)] = total.astype(BF)
+            return carry
+
+        lax.fori_loop(0, z_tiles, add, 0)
+        if k < dp_n:
+            send = copy(
+                part_z.at[k - 1], arrived_z.at[k - 1], z_send.at[k - 1], z_recv.at[k - 1], "dp", part
+            )
+            send.start()
+            z_sends.append(send)
+    for send in z_sends:
+        send.wait_recv()
+
+    weights = []
+    for k in range(dp_n):
+        origin = lax.rem(dp - k + dp_n, dp_n)
+        for source in range(exp_n):
+            name = ids_ref[origin * exp_n + source]
+            weights.append([jnp.where(name == a, 1.0, 0.0).astype(F32) for a in range(adapters)])
+
+    def combine(tile, carry):
+        totals = [jnp.zeros((16, 128), F32)] * adapters
+        for k in range(dp_n):
+            for source in range(exp_n):
+                ref = part_z.at[dp_n - 1] if k == 0 else arrived_z.at[k - 1]
+                value = ref[source, tile].astype(F32)
+                marks = weights[k * exp_n + source]
+                totals = [total + mark * value for total, mark in zip(totals, marks)]
+        for a in range(adapters):
+            table_ref[ctx, dp, a, tile] = totals[a].astype(BF)
+        return carry
+
+    lax.fori_loop(0, z_tiles, combine, 0)
+    az_sends, ax_sends = [], []
+    for k in range(1, dp_n):
+        send = copy(
+            table_ref.at[ctx, dp], table_ref.at[ctx, dp], az_send.at[k - 1], az_recv.at[k - 1],
+            "dp", lax.rem(dp + k, dp_n),
+        )
+        send.start()
+        az_sends.append(send)
+    for k in range(dp_n):
+        if k > 0:
+            az_sends[k - 1].wait_recv()
+        origin = lax.rem(dp - k + dp_n, dp_n)
+        for step in range(1, ctx_n):
+            send = copy(
+                table_ref.at[ctx, origin], table_ref.at[ctx, origin],
+                ax_send.at[step - 1, k], ax_recv.at[step - 1, k],
+                "context", lax.rem(ctx + step, ctx_n),
+            )
+            send.start()
+            ax_sends.append(send)
+    for send in ax_sends:
+        send.wait_recv()
+    for index in range(own_attn):
+        tile = tiles + index
+        where = (tile // x_tiles, (tile % x_tiles) // z_tiles, tile % x_tiles % z_tiles)
+        for a in range(adapters):
+            attn_table_ref[exp, index, a] = table_ref[where[0], where[1], a, where[2]]
+    last = []
+    for step in range(1, exp_n):
+        send = copy(
+            attn_table_ref.at[exp], attn_table_ref.at[exp], e_send.at[step - 1], e_recv.at[step - 1],
+            "expert", lax.rem(exp + step, exp_n),
+        )
+        send.start()
+        last.append(send)
+    for send in last:
+        send.wait()
+    for send in waits + z_sends + az_sends + ax_sends:
+        send.wait_send()
+
+
+def unpack_kernel(sizes, table_ref, attn_ref, down_ref, up_ref, in_down_ref, in_up_ref, out_down_ref, out_up_ref):
+    x_tiles, z_tiles, own_attn = sizes
+
+    def tile_at(tile):
+        local = tile % x_tiles
+        return table_ref[tile // x_tiles, local // z_tiles, 0, local % z_tiles].astype(F32)
+
+    tile = 0
+    for expert in range(in_up_ref.shape[1]):
+        for out_ref in (in_down_ref, in_up_ref, out_down_ref, out_up_ref):
+            rows, cols = out_ref.shape[2:]
+            for row in range(rows // 16):
+                for col in range(cols // 128):
+                    out_ref[0, expert, row * 16 : row * 16 + 16, col * 128 : col * 128 + 128] = tile_at(tile)
+                    tile += 1
+    tile = 0
+    for out_ref in (down_ref, up_ref):
+        rows, cols = out_ref.shape[1:]
+        for row in range(rows // 16):
+            for col in range(cols // 128):
+                out_ref[0, row * 16 : row * 16 + 16, col * 128 : col * 128 + 128] = attn_ref[
+                    tile // own_attn, tile % own_attn, 0
+                ].astype(F32)
+                tile += 1
+
+
+def reduce_adapters(adapter_ids, expert_grads, attn_down, attn_up, adapters):
+    ctx_n, dp_n, exp_n = (lax.axis_size(axis) for axis in ("context", "dp", "expert"))
+    experts = expert_grads[0].shape[1]
+    packed = jnp.concatenate(
+        [to_tiles(g)[:, e] for e in range(experts) for g in expert_grads], 1
+    ).astype(BF)
+    attn = jnp.concatenate([to_tiles(attn_down), to_tiles(attn_up)], 0).astype(BF)
+    tiles, attn_tiles = packed.shape[1], attn.shape[0]
+    own_attn = attn_tiles // exp_n
+    z_tiles = pl.cdiv(tiles + own_attn, ctx_n * dp_n)
+    x_tiles = z_tiles * dp_n
+    sizes = (ctx_n, dp_n, exp_n, adapters, tiles, attn_tiles, x_tiles, z_tiles)
+    dma = pltpu.SemaphoreType.DMA
+    many = max(ctx_n - 1, 1)
+    table, attn_table = pl.pallas_call(
+        functools.partial(reduce_kernel, sizes),
+        out_shape=(
+            jax.ShapeDtypeStruct((ctx_n, dp_n, adapters, z_tiles, 16, 128), BF),
+            jax.ShapeDtypeStruct((exp_n, own_attn, adapters, 16, 128), BF),
+        ),
+        in_specs=[
+            pl.BlockSpec(memory_space=pltpu.SMEM),
+            pl.BlockSpec(memory_space=pl.ANY),
+            pl.BlockSpec(memory_space=pltpu.VMEM),
+        ],
+        out_specs=(pl.BlockSpec(memory_space=pltpu.VMEM), pl.BlockSpec(memory_space=pltpu.VMEM)),
+        scratch_shapes=[
+            pltpu.VMEM((exp_n, ctx_n * x_tiles, 16, 128), BF),
+            pltpu.VMEM((many, dp_n, exp_n, z_tiles, 16, 128), BF),
+            pltpu.VMEM((dp_n, exp_n, z_tiles, 16, 128), BF),
+            pltpu.VMEM((max(dp_n - 1, 1), exp_n, z_tiles, 16, 128), BF),
+            dma, dma((exp_n,)), dma((exp_n,)), dma((many, dp_n)), dma((many, dp_n)),
+            dma((dp_n,)), dma((dp_n,)), dma((dp_n,)), dma((dp_n,)),
+            dma((many, dp_n)), dma((many, dp_n)), dma((exp_n,)), dma((exp_n,)),
+        ],
+        compiler_params=pltpu.CompilerParams(
+            collective_id=1, has_side_effects=True, vmem_limit_bytes=VLIMIT
+        ),
+        name="reduce_adapters",
+    )(adapter_ids, packed, attn)
+    shapes = [
+        (adapters,) + attn_down.shape,
+        (adapters,) + attn_up.shape,
+    ] + [(adapters,) + g.shape[1:] for g in expert_grads]
+    return pl.pallas_call(
+        functools.partial(unpack_kernel, (x_tiles, z_tiles, own_attn)),
+        grid=(adapters,),
+        out_shape=tuple(jax.ShapeDtypeStruct(shape, F32) for shape in shapes),
+        in_specs=[
+            pl.BlockSpec((ctx_n, dp_n, 1, z_tiles, 16, 128), lambda a: (0, 0, a, 0, 0, 0)),
+            pl.BlockSpec((exp_n, own_attn, 1, 16, 128), lambda a: (0, 0, a, 0, 0)),
+        ],
+        out_specs=tuple(
+            pl.BlockSpec((1,) + shape[1:], lambda a, n=len(shape): (a,) + (0,) * (n - 1))
+            for shape in shapes
+        ),
+        compiler_params=pltpu.CompilerParams(vmem_limit_bytes=VLIMIT),
+        name="unpack_adapters",
+    )(table, attn_table)
 
 
 def local(
@@ -367,7 +611,7 @@
     d_branch = d_mid.astype(jnp.bfloat16)
     d_rank_out = (ADAPT_SCALE * bdot("td,rd->tr", d_branch, up_sel[3])).astype(jnp.bfloat16)
     grad_up_out = ADAPT_SCALE * bdot("tr,td->rd", rank_out, d_branch)
-    grad_down_out = bdot("td,tr->dr", attn_flat, d_rank_out)
+    grad_down_out = bdot("td,tr->rd", attn_flat, d_rank_out)
     d_attn = (
         (bdot("te,de->td", d_branch, w_out) + bdot("tr,dr->td", d_rank_out, down_sel[3]))
         .astype(jnp.bfloat16)
@@ -416,7 +660,7 @@
     ).astype(jnp.bfloat16)
     d_rank_qkv = (ADAPT_SCALE * bdot("tpd,prd->ptr", d_proj, up_sel[:3])).astype(jnp.bfloat16)
     grad_up_qkv = ADAPT_SCALE * bdot("ptr,tpd->prd", rank_qkv, d_proj)
-    grad_down_qkv = bdot("td,ptr->pdr", normed_low, d_rank_qkv)
+    grad_down_qkv = bdot("td,ptr->prd", normed_low, d_rank_qkv)
     d_normed_one = bdot("te,de->td", d_proj.reshape(tok_count, 3 * model_dim), w_qkv) + bdot(
         "ptr,pdr->td", d_rank_qkv, down_sel[:3]
     )
@@ -428,23 +672,23 @@
         * (inv_one * inv_one * inv_one)
         * jnp.mean(scaled_one * resid_in, -1, keepdims=True)
     )
-    own_match = (jnp.arange(adapter_count, dtype=jnp.int32) == my_adapter).astype(jnp.float32)
-    down_table = (
-        own_match[:, None, None, None]
-        * jnp.concatenate([grad_down_qkv, grad_down_out[None]], 0)[None]
-    )
-    up_table = (
-        own_match[:, None, None, None] * jnp.concatenate([grad_up_qkv, grad_up_out[None]], 0)[None]
-    )
-    grad_attn_down, grad_attn_up = lax.psum((down_table, up_table), ("dp", "context", "expert"))
-    source_full = source_match.astype(jnp.float32)
-    part_in_down = fdot("ja,j...->a...", source_full, owner_grads[0])
-    part_in_up = fdot("ja,j...->a...", source_full, owner_grads[1])
-    part_out_down = fdot("ja,j...->a...", source_full, owner_grads[2])
-    part_out_up = fdot("ja,j...->a...", source_full, owner_grads[3])
-    grad_in_down, grad_in_up, grad_out_down, grad_out_up = lax.psum(
-        (part_in_down, part_in_up, part_out_down, part_out_up), ("dp", "context")
-    )
+    grad_down_all = jnp.concatenate([grad_down_qkv, grad_down_out[None]], 0)
+    grad_up_all = jnp.concatenate([grad_up_qkv, grad_up_out[None]], 0)
+    in_down, in_up, out_down, out_up = owner_grads
+    sources, experts, _, rank_dim, ffn_width = in_up.shape
+    sums = reduce_adapters(
+        adapter_ids,
+        (in_down, in_up.reshape(sources, experts, 2 * rank_dim, ffn_width), out_down, out_up),
+        grad_down_all.reshape(4 * rank_dim, model_dim),
+        grad_up_all.reshape(4 * rank_dim, model_dim),
+        adapter_count,
+    )
+    grad_attn_down = jnp.swapaxes(sums[0].reshape(adapter_count, 4, rank_dim, model_dim), 2, 3)
+    grad_attn_up = sums[1].reshape(adapter_count, 4, rank_dim, model_dim)
+    grad_in_down = jnp.swapaxes(sums[2], 2, 3)
+    grad_in_up = sums[3].reshape(adapter_count, experts, 2, rank_dim, ffn_width)
+    grad_out_down = jnp.swapaxes(sums[4], 2, 3)
+    grad_out_up = sums[5]
     return (
         layer_out.astype(jnp.bfloat16)[None],
         grad_in[None],

time: 1000 us -> 741 us (0.74)
  waiting for transfers between devices: 457 us -> 68.2 us
  Pallas kernels: 0 us -> 153 us
  matrix products: 256 us -> 233 us
    psum x2 -> x0, waiting for transfers between devices: 391 us -> none  [the longest x1 260 us: local(): lax.psum((part_in_down, part_in_up, part_out_down, part_out_up), ('dp', '...]
    pallas_call x0 -> x2, Pallas kernels: none -> 153 us  [the longest x1 144 us: reduce_adapters(): pl.pallas_call(functools.partial(reduce_kernel, sizes), out_shape=(jax.Sh...]
    reduce_scatter x1, waiting for transfers between devices: 1.53 us -> 27.5 us  [local(): lax.psum_scatter(d_key_all.astype(jnp.bfloat16), 'context', scatter_dimen...]
    reduce_scatter x1, waiting for transfers between devices: 26.2 us -> 3.13 us  [local(): lax.psum_scatter(d_value_all.astype(jnp.bfloat16), 'context', scatter_dim...]
    dot_general x9 -> x5, matrix products: 18.5 us -> 6.25 us  [fdot(): jnp.einsum(form, left, right, precision=HIGH, preferred_element_type=jnp....]
    dot_general x58, matrix products: 237 us -> 227 us  [bdot(): return jnp.einsum(form, left, right, preferred_element_type=jnp.float32)]
    unnamed x214 -> x216, local copies, waits for them, and re-layouts: 34 us -> 23.8 us
  transfers between devices with their start and end apart: 10 -> 8, of which waited for: 7 -> 5; matrix products, arithmetic and copies ran while one was open for 17% -> 18% of each run, Pallas kernels for 0% -> 0%
where the time goes in v1:
time: 741 us; the launch traced here: 733 us
  matrix products  233 us (31%)
  local copies, waits for them, and re-layouts  156 us (21%)
  Pallas kernels  153 us (21%)
  other arithmetic  79.2 us (11%)
  waiting for transfers between devices  68.2 us (9%)
  starting transfers between devices  21.8 us (3%)
  between operations  17.5 us (2%)
    dot_general x58, matrix products, bdot(): return jnp.einsum(form, left, right, preferred_element_type=jnp.float32)  227 us
    pallas_call x1, Pallas kernels, reduce_adapters(): pl.pallas_call(functools.partial(reduce_kernel, sizes), out_shape=(jax.Sh...  144 us
    reduce_scatter x1, waiting for transfers between devices, local(): lax.psum_scatter(d_key_all.astype(jnp.bfloat16), 'context', scatter_dimen...  27.5 us
    unnamed x216, local copies, waits for them, and re-layouts  23.8 us
    all_to_all x1, waiting for transfers between devices, local(): lax.all_to_all(d_outgoing, 'expert', split_axis=0, concat_axis=0, tiled=T...  19.3 us
    broadcast_in_dim x6, local copies, waits for them, and re-layouts, local(): jnp.where((route_tok == ffn_count + 2 + const_index)[:, :, None], const_t...  18.9 us
  transfers between devices with their start and end apart: 8, of which 5 were waited for; matrix products, arithmetic and copies ran while one was open for 18% of the time, Pallas kernels for 0%

profile of v1, /device:TPU:25, one launch (start us, length us, event | category | flops | bytes accessed | tf_op | source)
XLA Modules:
  0.0 733.1 jit_solution(14013805284828623531)
XLA Ops:
  7.3 5.9 copy.242
  61.0 5.4 mul.765
  72.1 31.1 %while.50 = (s32[]{:T(128)}, f32[12,512]{1,0:T(8,128)S(1)}, f32[12,512]{1,0:T(8,128)S(1)}, s32[1,512]{1,0:T(1,128)S(1)}, s32[1024]{0:T(1024)S(1)}, /*index=5*/bf...) while((s32[]{:T(128)}, f32[12,512]{1,0:T(8,128)S(1)}, ...), condition=%wide.region_4.5_spmd.clone, body=%wide.region_1.4_spmd.clone.sunk | while | flops 425491456 | bytes 27861188 | solution.py:471
  72.7 7.9 %fusion.320 = (f32[12,512]{1,0:T(8,128)S(1)}, f32[12,512,512]{2,1,0:T(8,128)}) fusion(pred[512,512]{0,1:T(8,128)(4,1)S(1)} %compare_and_fusion.6, bf16[512,12,64]{0,2,1:T(8,128)(2,1)S(1)} %get-tuple-element.1097, bf16[1024,12,64]{0,2,1:T(8,128)(2,1)} %get-tuple-element.1096, s32[]{:T(128)S(6)} %select_n.224), kind=kOutput, calls=%fused_computation.9.clone.1 | convolution fusion | flops 412084224 | bytes 14442500 | tf_op jit(solution)/shard_map/while/body/eval_jaxpr/qhd,khd->hqk/dot_general | solution.py:45
  80.6 7.1 exponential_reduce_fusion.2
  88.2 7.8 %fusion.320 = (f32[12,512]{1,0:T(8,128)S(1)}, f32[12,512,512]{2,1,0:T(8,128)}) fusion(pred[512,512]{0,1:T(8,128)(4,1)S(1)} %compare_and_fusion.6, bf16[512,12,64]{0,2,1:T(8,128)(2,1)S(1)} %get-tuple-element.1097, bf16[1024,12,64]{0,2,1:T(8,128)(2,1)} %get-tuple-element.1096, s32[]{:T(128)S(6)} %select_n.224), kind=kOutput, calls=%fused_computation.9.clone.1 | convolution fusion | flops 412084224 | bytes 14442500 | tf_op jit(solution)/shard_map/while/body/eval_jaxpr/qhd,khd->hqk/dot_general | solution.py:45
  96.0 7.1 exponential_reduce_fusion.2
  103.2 45.2 %while.51 = (s32[]{:T(128)}, f32[512,12,64]{0,2,1:T(8,128)}, f32[512,12,64]{0,2,1:T(8,128)}, bf16[1024,12,64]{0,2,1:T(8,128)(2,1)}, s32[1,512]{1,0:T(1,128)S(1)}...) while((s32[]{:T(128)}, f32[512,12,64]{0,2,1:T(8,128)}, ...), condition=%wide.region_6.7_spmd.clone, body=%wide.region_5.6_spmd.clone.sunk | while | flops 1244922880 | bytes 117252432 | solution.py:491
  103.2 7.5 %fusion.327 = f32[12,512,512]{2,1,0:T(8,128)} fusion(bf16[512,12,64]{0,2,1:T(8,128)(2,1)S(1)} %get-tuple-element.1138, bf16[1024,12,64]{0,2,1:T(8,128)(2,1)} %get-tuple-element.1137, s32[]{:T(128)S(6)} %select_n.227), kind=kOutput, calls=%fused_computation.34.clone.1 | convolution fusion | flops 402653184 | bytes 14155780 | tf_op jit(solution)/shard_map/while/body/eval_jaxpr/qhd,khd->hqk/dot_general | solution.py:45
  111.2 9.4 %bitcast_add_fusion.11 = f32[512,12,64]{0,2,1:T(8,128)} fusion(f32[512,12,64]{0,2,1:T(8,128)} %get-tuple-element.1118, f32[12,512,512]{2,1,0:T(8,128)} %fusion.327, f32[12,512]{1,0:T(8,128)S(1)} %get-tuple-element.1139, pred[512,512]{0,1:T(8,128)(4,1)S(1)} %compare_and_fusion.7, pred[]{:T(512)S(6)} %compare.10, ...), kind=kOutput, calls=%fused_computation.32.clone.1 | convolution fusion | flops 416022528 | bytes 16801796 | tf_op jit(solution)/shard_map/while/body/eval_jaxpr/hqk,khd->qhd/dot_general | solution.py:45
  125.4 7.5 %fusion.327 = f32[12,512,512]{2,1,0:T(8,128)} fusion(bf16[512,12,64]{0,2,1:T(8,128)(2,1)S(1)} %get-tuple-element.1138, bf16[1024,12,64]{0,2,1:T(8,128)(2,1)} %get-tuple-element.1137, s32[]{:T(128)S(6)} %select_n.227), kind=kOutput, calls=%fused_computation.34.clone.1 | convolution fusion | flops 402653184 | bytes 14155780 | tf_op jit(solution)/shard_map/while/body/eval_jaxpr/qhd,khd->hqk/dot_general | solution.py:45
  133.3 9.8 %bitcast_add_fusion.11 = f32[512,12,64]{0,2,1:T(8,128)} fusion(f32[512,12,64]{0,2,1:T(8,128)} %get-tuple-element.1118, f32[12,512,512]{2,1,0:T(8,128)} %fusion.327, f32[12,512]{1,0:T(8,128)S(1)} %get-tuple-element.1139, pred[512,512]{0,1:T(8,128)(4,1)S(1)} %compare_and_fusion.7, pred[]{:T(512)S(6)} %compare.10, ...), kind=kOutput, calls=%fused_computation.32.clone.1 | convolution fusion | flops 416022528 | bytes 16801796 | tf_op jit(solution)/shard_map/while/body/eval_jaxpr/hqk,khd->qhd/dot_general | solution.py:45
  157.6 4.6 reshape.801
  162.3 7.0 scatter_custom_fusion
  169.3 6.2 all-to-all-start
  184.4 10.4 %all-to-all-done = bf16[4,2,128,768]{3,2,1,0:T(8,128)(2,1)} async-done(((bf16[4,2,128,768]{3,2,1,0:T(8,128)(2,1)}), bf16[4,2,128,768]{3,2,1,0:T(8,128)(2,1)}, u32[]{:S(2)}, u32[]{:S(2)}) %all-to-all-start) | async-done | bytes 1572896 | tf_op jit(solution)/shard_map/all_to_all | solution.py:543
  196.8 15.0 %fusion.58 = f32[4,2,128,4096]{3,2,0,1:T(8,128)} fusion(bf16[2,768,4096]{2,1,0:T(8,128)(2,1)} %param.43, bf16[4,2,128,768]{3,2,1,0:T(8,128)(2,1)} %all-to-all-done), kind=kOutput, calls=%fused_computation.77 | convolution fusion | flops 6442450944 | bytes 30932992 | tf_op jit(solution)/shard_map/jecd,edf->jecf/dot_general | solution.py:45
  211.8 4.9 slice_add_fusion.1
  216.8 10.5 %multiply_convert_fusion = (bf16[4,2,128,2048]{3,2,0,1:T(8,128)(2,1)S(1)}, f32[4,2,128,2048]{3,2,0,1:T(8,128)}) fusion(f32[4,2,128,2048]{3,2,0,1:T(8,128)S(1)} %slice_add_fusion.1, bf16[4,2,16,2048]{3,0,2,1:T(4,128)(2,1)S(1)} %copy-done.56, bf16[4,2,128,16]{2,3,1,0:T(8,128)(2,1)S(1)} %get-tuple-element.830, f32[4,2,128,4096]{3,2,0,1:T(8,128)} %fusion.58), kind=kOutput, calls=%fused_computation.89 | convolution fusion | flops 83886080 | bytes 29917184 | tf_op jit(solution)/shard_map/jecr,jerf->jecf/dot_general | solution.py:45
  234.1 5.6 all-to-all-start.1
  246.8 5.3 broadcast_in_dim.322
  256.2 5.3 broadcast_in_dim.319
  265.7 5.3 broadcast_in_dim.315
  271.7 7.2 gather_fusion
  278.9 5.9 multiply_reduce_fusion
  285.5 7.6 %scatter_custom_fusion.1 = bf16[1024,768]{1,0:T(8,128)(2,1)} fusion(s32[1024]{0:T(1024)} %bitcast.516, f32[1024,768]{1,0:T(8,128)} %mul.765, f32[1024]{0:T(1024)S(1)} %mul.800, bf16[]{:T(256)} %constant.226.clone.1), kind=kCustom, calls=%fused_computation.143 | custom fusion | flops 1572864 | bytes 4723200 | tf_op jit(solution)/shard_map/scatter | solution.py:591
  293.1 4.5 all-to-all-start.2
  297.7 19.3 %all-to-all-done.2 = bf16[4,2,128,768]{3,2,1,0:T(8,128)(2,1)} async-done(((bf16[4,2,128,768]{3,2,1,0:T(8,128)(2,1)}), bf16[4,2,128,768]{3,2,1,0:T(8,128)(2,1)}, u32[]{:S(2)}, u32[]{:S(2)}) %all-to-all-start.2) | async-done | bytes 1572896 | tf_op jit(solution)/shard_map/all_to_all | solution.py:594
  319.1 10.2 %fusion.70 = f32[2,4,128,2048]{3,2,1,0:T(8,128)} fusion(bf16[2,2048,768]{2,1,0:T(8,128)(2,1)} %param.44, bf16[4,2,128,768]{3,2,1,0:T(8,128)(2,1)} %all-to-all-done.2), kind=kOutput, calls=%fused_computation.92 | convolution fusion | flops 3221225472 | bytes 16252928 | tf_op jit(solution)/shard_map/jecd,efd->jecf/dot_general | solution.py:45
  329.3 9.8 %fusion.63 = (bf16[4,2,128,2048]{3,2,0,1:T(8,128)(2,1)S(1)}, bf16[4,2,128,2048]{3,2,0,1:T(8,128)(2,1)}) fusion(f32[4,2,128,2048]{3,2,0,1:T(8,128)} %get-tuple-element.853, f32[4,2,128,2048]{3,2,0,1:T(8,128)S(1)} %bitcast.460, bf16[4,2,2048,16]{2,0,3,1:T(4,128)(2,1)S(1)} %copy-done.55, bf16[4,2,128,16]{2,3,1,0:T(8,128)(2,1)S(1)} %fusion.140, ...), kind=kOutput, calls=%fused_computation.80 | convolution fusion | flops 100663296 | bytes 34111488 | tf_op jit(solution)/shard_map/jecr,jefr->jecf/dot_general | solution.py:45
  339.1 5.0 fusion.76
  347.7 14.1 %fusion.86 = bf16[4,2,128,768]{3,2,0,1:T(8,128)(2,1)} fusion(f32[4,2,128,768]{3,2,0,1:T(8,128)} %fusion.167, bf16[2,768,4096]{2,1,0:T(8,128)(2,1)} %param.43, bf16[4,2,128,2048]{3,2,0,1:T(8,128)(2,1)} %get-tuple-element.806, bf16[4,2,128,2048]{3,2,0,1:T(8,128)(2,1)} %copy-done.27), kind=kOutput, calls=%fused_computation.111 | convolution fusion | flops 6460801024 | bytes 25690112 | tf_op jit(solution)/shard_map/jecf,edf->jecd/dot_general | solution.py:45
  364.5 5.2 all-to-all-start.3
  369.8 4.7 gather.11
  381.2 7.8 %all-to-all-done.3 = bf16[4,2,128,768]{3,2,1,0:T(8,128)(2,1)} async-done(((bf16[4,2,128,768]{3,2,1,0:T(8,128)(2,1)}), bf16[4,2,128,768]{3,2,1,0:T(8,128)(2,1)}, u32[]{:S(2)}, u32[]{:S(2)}) %all-to-all-start.3) | async-done | bytes 1572896 | tf_op jit(solution)/shard_map/all_to_all | solution.py:596
  392.3 7.7 %gather_fusion.1 = f32[1024,768]{1,0:T(8,128)} fusion(f32[1024,768]{1,0:T(8,128)} %bitcast_convert_fusion, s32[1024]{0:T(1024)S(1)} %copy-done.80), kind=kCustom, calls=%fused_computation.1 | custom fusion | bytes 6295552 | tf_op jit(solution)/shard_map/gather | solution.py:600
  400.1 5.2 gather.13
  405.3 14.6 %select_reduce_fusion = (f32[512,768]{1,0:T(8,128)S(1)}, f32[512,768]{1,0:T(8,128)S(1)}) fusion(f32[512,2,768]{2,1,0:T(2,128)} %gather.13, pred[512,2]{1,0:T(8,128)(4,1)S(1)} %copy-done.52, f32[512,768]{1,0:T(8,128)} %copy-done.13, pred[512,2]{1,0:T(8,128)(4,1)S(1)} %copy-done.46, f32[512,768]{1,0:T(8,128)} %get-tuple-element.861, ...), kind=kLoop, calls=%fused_computation.114 | loop fusion | flops 8650752 | bytes 12591104 | tf_op jit(solution)/shard_map/reduce_sum | solution.py:602
  431.8 59.7 %while.52 = (s32[]{:T(128)}, f32[512,12,64]{0,2,1:T(8,128)}, bf16[1024,12,64]{0,2,1:T(8,128)(2,1)}, bf16[1024,12,64]{0,2,1:T(8,128)(2,1)}, bf16[1024,12,64]{0,2,...) while((s32[]{:T(128)}, f32[512,12,64]{0,2,1:T(8,128)}, ...), condition=%wide.region_35.36_spmd.clone, body=%wide.region_34.35_spmd.clone.sunk | while | flops 2047083520 | bytes 176275920 | solution.py:645
  439.8 6.2 fusion.339
  446.0 5.4 bitcast_add_fusion.13
  453.5 6.9 bitcast_dynamic-update-slice_fusion.5
  469.2 6.2 fusion.339
  475.4 5.9 bitcast_add_fusion.13
  483.3 7.0 bitcast_dynamic-update-slice_fusion.5
  519.3 27.5 %reduce-scatter.3.cloned.1.call-done = bf16[512,12,64]{0,2,1:T(8,128)(2,1)} async-done(((bf16[1024,12,64]{0,2,1:T(8,128)(2,1)}), bf16[512,12,64]{0,2,1:T(8,128)(2,1)}) %reduce-scatter.3.cloned.1.call-update) | async-done | bytes 786448 | tf_op jit(solution)/shard_map/reduce_scatter | solution.py:649
  573.4 144.1 %reduce_adapters.1 = (bf16[2,4,8,18,16,128]{5,4,3,2,1,0:T(8,128)(2,1)}, bf16[4,12,8,16,128]{4,3,2,1,0:T(8,128)(2,1)}) custom-call(s32[16]{0:T(128)} %ids_ref.1, bf16[4,132,16,128]{3,2,1,0:T(8,128)(2,1)} %fusion.182.grads_ref, bf16[48,16,128]{2,1,0:T(8,128)(2,1)} %pad_maximum_fusion.4.attn_ref), custom_call_target="tpu_custom_call" | custom-call | tf_op jit(solution)/shard_map/reduce_adapters/pallas_call | solution.py:339
  717.6 8.7 %unpack_adapters.1 = (f32[8,64,768]{2,1,0:T(8,128)}, f32[8,64,768]{2,1,0:T(8,128)}, f32[8,2,32,768]{3,2,1,0:T(8,128)}, f32[8,2,32,2048]{3,2,1,0:T(8,128)}, f32[8...) custom-call(bf16[2,4,8,18,16,128]{5,4,3,2,1,0:T(8,128)(2,1)} %get-tuple-element.550.table_ref, ...), custom_call_target="tpu_custom_call" | custom-call | tf_op jit(solution)/shard_map/unpack_adapters/pallas_call | solution.py:369
  (460 shorter events, 212.0 us)
Async XLA Ops:
  7.2 46.4 %copy-start = (bf16[8,2,2,16,2048]{4,3,2,1,0:T(8,128)(2,1)S(1)}, bf16[8,2,2,16,2048]{4,3,2,1,0:T(8,128)(2,1)}, u32[]{:S(2)}) copy-start(bf16[8,2,2,16,2048]{4,3,2,1,0:T(8,128)(2,1)} %param.46) | copy-start | bytes 6291460
  7.2 64.8 %all-gather.6.cloned.1.call-start = ((), (), s32[]{:S(2)}) async-start(), calls=%async_computation.7 | async-start | bytes 2359296 | tf_op jit(solution)/shard_map/all_gather | solution.py:445
  13.2 7.5 %copy-start.78 = (f32[768]{0:T(1024)}, f32[768]{0:T(1024)S(1)}, u32[]{:S(2)}) copy-start(f32[768]{0:T(1024)S(1)} %convert_element_type.229) | copy-start | bytes 9220
  38.7 8.8 %copy-start.104 = (bf16[768]{0:T(1024)(128)(2,1)S(1)}, bf16[768]{0:T(1024)(128)(2,1)}, u32[]{:S(2)}) copy-start(bf16[768]{0:T(1024)(128)(2,1)} %param.38) | copy-start | bytes 4612
  38.7 64.5 %all-gather.4.cloned.1.call-start = ((), (), s32[]{:S(2)}) async-start(), calls=%async_computation.6 | async-start | bytes 2359296 | tf_op jit(solution)/shard_map/all_gather | solution.py:446
  44.1 24.0 %copy-start.90 = (pred[512,2]{0,1:T(4,128)(4,1)}, pred[512,2]{0,1:T(4,128)(4,1)S(1)}, u32[]{:S(2)}) copy-start(pred[512,2]{0,1:T(4,128)(4,1)S(1)} %get-tuple-element.840) | copy-start | bytes 3076
  44.1 24.9 %copy-start.88 = (pred[512,2]{0,1:T(4,128)(4,1)}, pred[512,2]{0,1:T(4,128)(4,1)S(1)}, u32[]{:S(2)}) copy-start(pred[512,2]{0,1:T(4,128)(4,1)S(1)} %get-tuple-element.839) | copy-start | bytes 3076
  44.1 25.9 %copy-start.86 = (pred[512,2]{0,1:T(4,128)(4,1)}, pred[512,2]{0,1:T(4,128)(4,1)S(1)}, u32[]{:S(2)}) copy-start(pred[512,2]{0,1:T(4,128)(4,1)S(1)} %get-tuple-element.838) | copy-start | bytes 3076
  61.0 11.0 %copy-start.34 = (bf16[512,12,32]{0,2,1:T(8,128)(2,1)S(1)}, bf16[512,12,32]{0,2,1:T(8,128)(2,1)}, u32[]{:S(2)}) copy-start(bf16[512,12,32]{0,2,1:T(8,128)(2,1)} %get-tuple-element.815) | copy-start | bytes 1179652
  61.0 11.0 %copy-start.35 = (bf16[512,12,32]{0,2,1:T(8,128)(2,1)S(1)}, bf16[512,12,32]{0,2,1:T(8,128)(2,1)}, u32[]{:S(2)}) copy-start(bf16[512,12,32]{0,2,1:T(8,128)(2,1)} %get-tuple-element.816) | copy-start | bytes 1179652
  67.5 94.8 %copy-start.101 = (s32[1024,1]{0,1:T(1,128)}, s32[1024,1]{0,1:T(1,128)S(1)}, u32[]{:S(2)}) copy-start(s32[1024,1]{0,1:T(1,128)S(1)} %get-tuple-element.832) | copy-start | bytes 12292
  111.1 9.4 %copy-start.4 = (f32[12,512,512]{2,1,0:T(8,128)S(1)}, f32[12,512,512]{2,1,0:T(8,128)}, u32[]{:S(2)}) copy-start(f32[12,512,512]{2,1,0:T(8,128)} %fusion.327) | copy-start | bytes 37748740 | tf_op jit(solution)/shard_map/while
  111.1 9.4 %copy-start.38 = (f32[512,12,64]{0,2,1:T(8,128)S(1)}, f32[512,12,64]{0,2,1:T(8,128)}, u32[]{:S(2)}) copy-start(f32[512,12,64]{0,2,1:T(8,128)} %get-tuple-element.1119) | copy-start | bytes 4718596 | tf_op jit(solution)/shard_map/while
  111.1 9.4 %copy-start.106 = (bf16[1024,12,64]{0,2,1:T(8,128)(2,1)S(1)}, bf16[1024,12,64]{0,2,1:T(8,128)(2,1)}, u32[]{:S(2)}) copy-start(bf16[1024,12,64]{0,2,1:T(8,128)(2,1)} %get-tuple-element.1134) | copy-start | bytes 4718596 | tf_op jit(solution)/shard_map/while
  133.3 9.8 %copy-start.4 = (f32[12,512,512]{2,1,0:T(8,128)S(1)}, f32[12,512,512]{2,1,0:T(8,128)}, u32[]{:S(2)}) copy-start(f32[12,512,512]{2,1,0:T(8,128)} %fusion.327) | copy-start | bytes 37748740 | tf_op jit(solution)/shard_map/while
  133.3 9.8 %copy-start.38 = (f32[512,12,64]{0,2,1:T(8,128)S(1)}, f32[512,12,64]{0,2,1:T(8,128)}, u32[]{:S(2)}) copy-start(f32[512,12,64]{0,2,1:T(8,128)} %get-tuple-element.1119) | copy-start | bytes 4718596 | tf_op jit(solution)/shard_map/while
  133.3 9.8 %copy-start.106 = (bf16[1024,12,64]{0,2,1:T(8,128)(2,1)S(1)}, bf16[1024,12,64]{0,2,1:T(8,128)(2,1)}, u32[]{:S(2)}) copy-start(bf16[1024,12,64]{0,2,1:T(8,128)(2,1)} %get-tuple-element.1134) | copy-start | bytes 4718596 | tf_op jit(solution)/shard_map/while
  162.3 13.2 %copy-start.85 = (bf16[2,768,2]{1,2,0:T(2,128)(2,1)S(1)}, bf16[2,768,2]{1,2,0:T(2,128)(2,1)}, u32[]{:S(2)}) copy-start(bf16[2,768,2]{1,2,0:T(2,128)(2,1)} %param.41) | copy-start | bytes 18436
  169.3 25.4 %all-to-all-start = ((bf16[4,2,128,768]{3,2,1,0:T(8,128)(2,1)}), bf16[4,2,128,768]{3,2,1,0:T(8,128)(2,1)}, u32[]{:S(2)}, u32[]{:S(2)}) async-start(bf16[4,2,128,768]{3,2,1,0:T(8,128)(2,1)} %bitcast.464), calls=%async_computation | async-start | bytes 3145728 | tf_op jit(solution)/shard_map/all_to_all | solution.py:543
  180.2 14.5 %copy-start.33 = (bf16[4,2,768,32]{2,0,3,1:T(4,128)(2,1)S(1)}, bf16[4,2,768,32]{2,0,3,1:T(4,128)(2,1)}, u32[]{:S(2)}) copy-start(bf16[4,2,768,32]{2,0,3,1:T(4,128)(2,1)} %convolution_convert_fusion.3) | copy-start | bytes 1179652
  196.8 15.1 %copy-start.64 = (bf16[4,2,128,32]{2,3,1,0:T(8,128)(2,1)}, bf16[4,2,128,32]{2,3,1,0:T(8,128)(2,1)S(1)}, u32[]{:S(2)}) copy-start(bf16[4,2,128,32]{2,3,1,0:T(8,128)(2,1)S(1)} %convolution_convert_fusion.6) | copy-start | bytes 196612
  211.8 17.5 %slice-start.2 = ((s8[6291456]{0:T(1024)(128)(4,1)}), s8[4194304]{0:T(1024)(128)(4,1)S(1)}, s32[]{:S(2)}) async-start(s8[6291456]{0:T(1024)(128)(4,1)} %bitcast.517), calls=%async_computation.12 | async-start | bytes 8388608
  216.7 10.5 %copy-start.18 = (f32[4,2,128,2048]{3,2,0,1:T(8,128)}, f32[4,2,128,2048]{3,2,0,1:T(8,128)S(1)}, u32[]{:S(2)}) copy-start(f32[4,2,128,2048]{3,2,0,1:T(8,128)S(1)} %slice_add_fusion.1) | copy-start | bytes 25165828
  216.8 10.5 %copy-start.54 = (bf16[4,2,2048,16]{2,0,3,1:T(4,128)(2,1)S(1)}, bf16[4,2,2048,16]{2,0,3,1:T(4,128)(2,1)}, u32[]{:S(2)}) copy-start(bf16[4,2,2048,16]{2,0,3,1:T(4,128)(2,1)} %convolution_convert_fusion.1) | copy-start | bytes 1572868
  216.8 12.6 %slice-start.3 = ((s8[6291456]{0:T(1024)(128)(4,1)}), s8[2097152]{0:T(1024)(128)(4,1)S(1)}, s32[]{:S(2)}) async-start(s8[6291456]{0:T(1024)(128)(4,1)} %bitcast.517), calls=%async_computation.13 | async-start | bytes 4194304
  234.1 37.5 %all-to-all-start.1 = ((bf16[4,2,128,768]{3,2,1,0:T(8,128)(2,1)}), bf16[4,2,128,768]{3,2,1,0:T(8,128)(2,1)}, u32[]{:S(2)}, u32[]{:S(2)}) async-start(bf16[4,2,128,768]{3,2,1,0:T(8,128)(2,1)} %copy.267), calls=%async_computation.1 | async-start | bytes 3145728 | tf_op jit(solution)/shard_map/all_to_all | solution.py:545
  293.1 23.9 %all-to-all-start.2 = ((bf16[4,2,128,768]{3,2,1,0:T(8,128)(2,1)}), bf16[4,2,128,768]{3,2,1,0:T(8,128)(2,1)}, u32[]{:S(2)}, u32[]{:S(2)}) async-start(bf16[4,2,128,768]{3,2,1,0:T(8,128)(2,1)} %bitcast.466), calls=%async_computation.2 | async-start | bytes 3145728 | tf_op jit(solution)/shard_map/all_to_all | solution.py:594
  317.0 12.3 %slice-start = ((s8[8388608]{0:T(1024)(128)(4,1)}), s8[4194304]{0:T(1024)(128)(4,1)S(1)}, s32[]{:S(2)}) async-start(s8[8388608]{0:T(1024)(128)(4,1)} %bitcast.459), calls=%async_computation.10 | async-start | bytes 8388608
  319.1 10.2 %copy-start.72 = (bf16[4,2,128,16]{2,3,1,0:T(8,128)(2,1)}, bf16[4,2,128,16]{2,3,1,0:T(8,128)(2,1)S(1)}, u32[]{:S(2)}) copy-start(bf16[4,2,128,16]{2,3,1,0:T(8,128)(2,1)S(1)} %fusion.140) | copy-start | bytes 98308
  319.1 10.2 %slice-start.1 = ((s8[8388608]{0:T(1024)(128)(4,1)}), s8[4194304]{0:T(1024)(128)(4,1)S(1)}, s32[]{:S(2)}) async-start(s8[8388608]{0:T(1024)(128)(4,1)} %bitcast.459), calls=%async_computation.11 | async-start | bytes 8388608
  319.1 10.2 %copy-start.55 = (bf16[4,2,2048,16]{2,0,3,1:T(4,128)(2,1)S(1)}, bf16[4,2,2048,16]{2,0,3,1:T(4,128)(2,1)}, u32[]{:S(2)}) copy-start(bf16[4,2,2048,16]{2,0,3,1:T(4,128)(2,1)} %convolution_convert_fusion.1) | copy-start | bytes 1572868
  329.3 9.8 %copy-start.57 = (bf16[4,2,16,2048]{3,0,2,1:T(4,128)(2,1)S(1)}, bf16[4,2,16,2048]{3,0,2,1:T(4,128)(2,1)}, u32[]{:S(2)}) copy-start(bf16[4,2,16,2048]{3,0,2,1:T(4,128)(2,1)} %get-tuple-element.822) | copy-start | bytes 1572868
  345.3 16.4 %copy-start.62 = (f32[4,2,128,16]{2,3,1,0:T(8,128)}, f32[4,2,128,16]{2,3,1,0:T(8,128)S(1)}, u32[]{:S(2)}) copy-start(f32[4,2,128,16]{2,3,1,0:T(8,128)S(1)} %fusion.80) | copy-start | bytes 196612
  364.5 24.5 %all-to-all-start.3 = ((bf16[4,2,128,768]{3,2,1,0:T(8,128)(2,1)}), bf16[4,2,128,768]{3,2,1,0:T(8,128)(2,1)}, u32[]{:S(2)}, u32[]{:S(2)}) async-start(bf16[4,2,128,768]{3,2,1,0:T(8,128)(2,1)} %copy.289), calls=%async_computation.3 | async-start | bytes 3145728 | tf_op jit(solution)/shard_map/all_to_all | solution.py:596
  369.7 148.2 %reduce-scatter.5.cloned.1.call-start = ((), (), s32[]{:S(2)}) async-start(), calls=%async_computation.9 | async-start | bytes 2359296 | tf_op jit(solution)/shard_map/reduce_scatter | solution.py:652
  405.3 14.6 %copy-start.11 = (f32[512,768]{1,0:T(8,128)S(1)}, f32[512,768]{1,0:T(8,128)}, u32[]{:S(2)}) copy-start(f32[512,768]{1,0:T(8,128)} %copy-done.10) | copy-start | bytes 4718596
  405.3 14.6 %copy-start.25 = (f32[512,768]{1,0:T(8,128)S(1)}, f32[512,768]{1,0:T(8,128)}, u32[]{:S(2)}) copy-start(f32[512,768]{1,0:T(8,128)} %fusion.207) | copy-start | bytes 4718596
  405.3 14.6 %copy-start.26 = (f32[512,768]{1,0:T(8,128)S(1)}, f32[512,768]{1,0:T(8,128)}, u32[]{:S(2)}) copy-start(f32[512,768]{1,0:T(8,128)} %fusion.200) | copy-start | bytes 4718596
  431.7 59.9 %copy-start.84 = (f32[12,12]{1,0:T(8,128)S(1)}, f32[12,12]{1,0:T(8,128)}, u32[]{:S(2)}) copy-start(f32[12,12]{1,0:T(8,128)} %param.40) | copy-start | bytes 1732
  431.7 60.8 %copy-start.65 = (bf16[4,2,128,32]{2,3,1,0:T(8,128)(2,1)S(1)}, bf16[4,2,128,32]{2,3,1,0:T(8,128)(2,1)}, u32[]{:S(2)}) copy-start(bf16[4,2,128,32]{2,3,1,0:T(8,128)(2,1)} %copy-done.64) | copy-start | bytes 196612
  432.1 7.7 %copy-start.107 = (bf16[1024,12,64]{0,2,1:T(8,128)(2,1)S(1)}, bf16[1024,12,64]{0,2,1:T(8,128)(2,1)}, u32[]{:S(2)}) copy-start(bf16[1024,12,64]{0,2,1:T(8,128)(2,1)} %get-tuple-element.1188) | copy-start | bytes 4718596 | tf_op jit(solution)/shard_map/while
  461.6 7.7 %copy-start.107 = (bf16[1024,12,64]{0,2,1:T(8,128)(2,1)S(1)}, bf16[1024,12,64]{0,2,1:T(8,128)(2,1)}, u32[]{:S(2)}) copy-start(bf16[1024,12,64]{0,2,1:T(8,128)(2,1)} %get-tuple-element.1188) | copy-start | bytes 4718596 | tf_op jit(solution)/shard_map/while
  491.5 55.3 %reduce-scatter.3.cloned.1.call-start = ((), (), s32[]{:S(2)}) async-start(), calls=%async_computation.8 | async-start | bytes 2359296 | tf_op jit(solution)/shard_map/reduce_scatter | solution.py:649
  514.7 33.4 %copy-start.5 = (f32[512,12,64]{0,2,1:T(8,128)S(1)}, f32[512,12,64]{0,2,1:T(8,128)}, u32[]{:S(2)}) copy-start(f32[512,12,64]{0,2,1:T(8,128)} %get-tuple-element.547) | copy-start | bytes 4718596
  514.7 33.4 %copy-start.44 = (f32[512,32]{0,1:T(8,128)S(1)}, f32[512,32]{0,1:T(8,128)}, u32[]{:S(2)}) copy-start(f32[512,32]{0,1:T(8,128)} %copy-done.43) | copy-start | bytes 196612
  514.7 33.4 %copy-start.59 = (f32[512,32]{0,1:T(8,128)S(1)}, f32[512,32]{0,1:T(8,128)}, u32[]{:S(2)}) copy-start(f32[512,32]{0,1:T(8,128)} %get-tuple-element.841) | copy-start | bytes 196612
  551.4 8.7 %copy-start.67 = (bf16[3,16,512]{2,1,0:T(8,128)(2,1)S(1)}, bf16[3,16,512]{2,1,0:T(8,128)(2,1)}, u32[]{:S(2)}) copy-start(bf16[3,16,512]{2,1,0:T(8,128)(2,1)} %copy-done.66) | copy-start | bytes 147460
  717.5 8.7 %copy-start.1 = (bf16[8,2,2,16,2048]{4,3,2,1,0:T(8,128)(2,1)S(1)}, bf16[8,2,2,16,2048]{4,3,2,1,0:T(8,128)(2,1)}, u32[]{:S(2)}) copy-start(bf16[8,2,2,16,2048]{4,3,2,1,0:T(8,128)(2,1)} %param.46) | copy-start | bytes 6291460
  (83 other events, 315.5 us)
Sparse Core Ops, SparseCore 0:
  38.8 28.1 all-gather.5
  69.1 27.1 all-gather.3
  491.6 26.2 reduce-scatter.4
  520.7 26.0 reduce-scatter.2

commit v2 on v1

--- a/solution.py
+++ b/solution.py
@@ -3,6 +3,7 @@
 
 import jax
 import jax.numpy as jnp
+import numpy as np
 from jax import lax
 from jax.experimental import pallas as pl
 from jax.experimental.pallas import tpu as pltpu
@@ -22,63 +23,12 @@
 HIGH = lax.Precision.HIGHEST
 
 
-def rotate(vectors, positions, direction):
-    half_dim = vectors.shape[-1] // 2
-    frequency = jnp.exp(
-        jnp.arange(half_dim).astype(jnp.float32) * (-2.0 * math.log(10000.0) / vectors.shape[-1])
-    )
-    angles = positions[:, None] * frequency[None, :]
-    cosine = jnp.cos(angles)[:, None, :]
-    sine_part = direction * jnp.sin(angles)[:, None, :]
-    first_half = vectors[..., :half_dim]
-    second_half = vectors[..., half_dim:]
-    return jnp.concatenate(
-        [
-            first_half * cosine - second_half * sine_part,
-            first_half * sine_part + second_half * cosine,
-        ],
-        -1,
-    )
-
-
 def bdot(form, left, right):
     return jnp.einsum(form, left, right, preferred_element_type=jnp.float32)
 
 
 def fdot(form, left, right):
     return jnp.einsum(form, left, right, precision=HIGH, preferred_element_type=jnp.float32)
-
-
-def masked_scores(queries, key_rows, query_pos, query_seg, key_pos, key_seg):
-    raw_scores = bdot("qhd,khd->hqk", queries, key_rows) * queries.shape[-1] ** (-0.5)
-    allowed = (query_seg[:, None] == key_seg[None, :]) & (key_pos[None, :] <= query_pos[:, None])
-    return jnp.where(allowed[None], raw_scores, NEG)
-
-
-def block_grads(
-    queries,
-    d_out,
-    log_total,
-    row_delta,
-    query_pos,
-    query_seg,
-    key_rows,
-    value_rows,
-    key_pos,
-    key_seg,
-):
-    probs_block = jnp.exp(
-        masked_scores(queries, key_rows, query_pos, query_seg, key_pos, key_seg)
-        - log_total[:, :, None]
-    )
-    rounded = probs_block.astype(jnp.bfloat16)
-    d_probs = bdot("qhd,khd->hqk", d_out, value_rows)
-    d_scores = (probs_block * (d_probs - row_delta[:, :, None])).astype(jnp.bfloat16)
-    score_scale = queries.shape[-1] ** (-0.5)
-    d_query = bdot("hqk,khd->qhd", d_scores, key_rows) * score_scale
-    d_key = bdot("hqk,qhd->khd", d_scores, queries) * score_scale
-    d_value = bdot("hqk,qhd->khd", rounded, d_out)
-    return (d_query, d_key, d_value)
 
 
 def expert_hidden(arrived, tables, w_gate_up, ffn_width):
@@ -145,6 +95,566 @@
         "jecr,jedr->jecd", d_rank_in, tables[0]
     )
     return (d_arrived, (grad_in_down, grad_in_up, grad_out_down, grad_out_up))
+
+
+def nt(left, right):
+    return lax.dot_general(left, right, (((1,), (1,)), ((), ())), preferred_element_type=F32)
+
+
+def tn(left, right):
+    return lax.dot_general(left, right, (((0,), (0,)), ((), ())), preferred_element_type=F32)
+
+
+def nn(left, right):
+    return jnp.dot(left, right, preferred_element_type=F32)
+
+
+def rope_tables(positions, width):
+    half = width // 2
+    frequency = np.exp(np.arange(half) * (-2.0 * math.log(10000.0) / width))
+    angles = np.arange(positions)[:, None] * frequency[None, :]
+    cosine, sine = np.cos(angles), np.sin(angles)
+    return (
+        np.concatenate([cosine] * 4, 1).astype(np.float32),
+        np.concatenate([-sine, sine] * 2, 1).astype(np.float32),
+    )
+
+
+def turn(block, cosine, sine, width):
+    half = width // 2
+    lane = lax.broadcasted_iota(jnp.int32, block.shape, 1)
+    other = jnp.where(
+        lane % width < half, pltpu.roll(block, 128 - half, 1), pltpu.roll(block, half, 1)
+    )
+    return block * cosine + other * sine
+
+
+def greet(axes):
+    barrier = pltpu.get_barrier_semaphore()
+    count = 0
+    for axis, size in axes:
+        index = lax.axis_index(axis)
+        for step in range(1, size):
+            pl.semaphore_signal(
+                barrier, inc=1, device_id={axis: lax.rem(index + step, size)}, device_id_type=MESH
+            )
+        count += size - 1
+    return lambda: pl.semaphore_wait(barrier, count)
+
+
+def remote(src, dst, send, recv, axis, target):
+    return pltpu.make_async_remote_copy(
+        src_ref=src, dst_ref=dst, send_sem=send, recv_sem=recv,
+        device_id={axis: target}, device_id_type=MESH,
+    )
+
+
+def blocks_of(ctx_n, ctx, count):
+    return [lax.rem(ctx + 1 + j, ctx_n) for j in range(count)]
+
+
+def fill_bias(bias_ref, seg_all, ctx_n, ctx, tok, count):
+    own = jnp.broadcast_to(seg_all[ctx, 0:1, :].astype(F32), (128, tok))
+    query_seg = jnp.transpose(own)[:, 0:1]
+    query_pos = ctx * tok + lax.broadcasted_iota(jnp.int32, (tok, tok), 0)
+    for j, block in enumerate([ctx] + blocks_of(ctx_n, ctx, count)):
+        key_seg = seg_all[block, 0:1, :].astype(F32)
+        key_pos = block * tok + lax.broadcasted_iota(jnp.int32, (tok, tok), 1)
+        allowed = (query_seg == key_seg) & (key_pos <= query_pos)
+        bias_ref[j] = jnp.where(allowed, 0.0, NEG).astype(bias_ref.dtype)
+
+
+def attention_kernel(
+    sizes, ids_ref, x_ref, seg_ref, mixed_ref, gain_one_ref, w_qkv_ref, w_out_ref, down_ref, up_ref,
+    gain_two_ref, router_ref, cos_ref, sin_ref,
+    q_ref, k_ref, v_ref, normed_ref, rank_ref, total_ref, flat_ref, rank_out_ref, mid_ref, rows_ref,
+    logits_ref, seg_all,
+    x_all, bias_ref, send_sem, recv_sem, seg_send, seg_recv,
+):
+    ctx_n, exp_n, rank = sizes
+    ctx = lax.axis_index("context")
+    sequence = lax.axis_index("dp") * exp_n + lax.axis_index("expert")
+    tok, model = x_ref.shape
+    pairs, head_dim = model // 128, 64
+    entered = greet([("context", ctx_n)])
+    seg_all[ctx] = jnp.broadcast_to(seg_ref[...], (8, tok))
+    if ctx_n > 1:
+        entered()
+        copies = []
+        for step in range(1, ctx_n):
+            peer = lax.rem(ctx + step, ctx_n)
+            copies.append(
+                (
+                    peer,
+                    step,
+                    remote(x_ref, x_all.at[ctx], send_sem.at[step - 1], recv_sem.at[step - 1], "context", peer),
+                    remote(seg_all.at[ctx], seg_all.at[ctx], seg_send.at[step - 1], seg_recv.at[step - 1], "context", peer),
+                )
+            )
+
+        def to_later(peer):
+            return ctx < peer if ctx_n == 2 else ctx < ctx_n
+
+        def from_earlier(step):
+            return lax.rem(ctx - step + ctx_n, ctx_n) < ctx if ctx_n == 2 else ctx < ctx_n
+
+        for peer, step, rows_copy, seg_copy in copies:
+            @pl.when(to_later(peer))
+            def _(rows_copy=rows_copy, seg_copy=seg_copy):
+                seg_copy.start()
+                rows_copy.start()
+
+    adapter = ids_ref[sequence]
+    down = down_ref[adapter]
+    up = up_ref[adapter]
+    gain_one = gain_one_ref[...].astype(F32)
+    column = lax.broadcasted_iota(jnp.int32, (tok, down.shape[0]), 1) // rank
+
+    def project(values, block, first):
+        wide = values.astype(F32)
+        inv = lax.rsqrt(jnp.mean(wide * wide, -1, keepdims=True) + EPSILON)
+        normed_ref[block] = (wide * inv * gain_one).astype(BF)
+        normed = normed_ref[block]
+        ranks = nt(normed, down).astype(BF)
+        rank_ref[block] = ranks
+        start = pl.multiple_of(block * tok, tok)
+        for p in range(first, 3):
+            part = jnp.where(column == p, ADAPT_SCALE * ranks.astype(F32), 0.0).astype(BF)
+
+            def chunk(i, carry, p=p, part=part):
+                wide_cols = pl.ds(pl.multiple_of(p * model + i * 256, 256), 256)
+                cols = pl.ds(pl.multiple_of(i * 256, 256), 256)
+                proj = nn(normed_ref[block], w_qkv_ref[:, wide_cols]) + nn(
+                    part, up_cols[:, cols]
+                )
+                for half in range(2):
+                    piece = proj[:, half * 128 : half * 128 + 128]
+                    if p < 2:
+                        piece = turn(
+                            piece, cos_ref[pl.ds(start, tok)], sin_ref[pl.ds(start, tok)], head_dim
+                        )
+                    if p == 0:
+                        q_ref[2 * i + half] = (piece * head_dim ** (-0.5)).astype(BF)
+                    else:
+                        (k_ref if p == 1 else v_ref)[block, 2 * i + half] = piece.astype(BF)
+                return carry
+
+            up_cols = up_ref.at[adapter]
+            lax.fori_loop(0, model // 256, chunk, 0)
+
+    project(x_ref[...], ctx, 0)
+    lane = lax.broadcasted_iota(jnp.int32, (1, 128), 1)
+    marks = [(lane < 64), (lane >= 64)]
+    half_rows = tok // 2
+
+    def attend(count):
+        fill_bias(bias_ref, seg_all, ctx_n, ctx, tok, count)
+        others = blocks_of(ctx_n, ctx, count)
+
+        def pair(i, carry):
+            for half in range(2):
+                rows = slice(half * half_rows, (half + 1) * half_rows)
+                own_width = (half + 1) * half_rows
+                q = q_ref[i, rows]
+                result = jnp.zeros((half_rows, 128), F32)
+                stats = total_ref[rows]
+                for head in range(2):
+                    mark = marks[head]
+                    q_head = jnp.where(mark, q, 0)
+                    scores = [
+                        nt(q_head, k_ref[ctx, i, 0:own_width]) + bias_ref[0, rows, 0:own_width]
+                    ]
+                    for j, block in enumerate(others):
+                        scores.append(nt(q_head, k_ref[block, i]) + bias_ref[j + 1, rows])
+                    top = functools.reduce(
+                        jnp.maximum, [jnp.max(s, -1, keepdims=True) for s in scores]
+                    )
+                    exps = [jnp.exp(s - top) for s in scores]
+                    total = functools.reduce(jnp.add, [jnp.sum(e, -1, keepdims=True) for e in exps])
+                    stats = jnp.where(lane == 2 * i + head, top + jnp.log(total), stats)
+                    inv = 1.0 / total
+                    for e, block in zip(exps, [ctx] + others):
+                        v = k_v(block, i, e.shape[1])
+                        result = result + nn((e * inv).astype(BF), jnp.where(mark, v, 0))
+                total_ref[rows] = stats
+                flat_ref[rows, pl.ds(pl.multiple_of(i * 128, 128), 128)] = result.astype(BF)
+            return carry
+
+        def k_v(block, i, width):
+            return v_ref[block, i, 0:width]
+
+        lax.fori_loop(0, pairs, pair, 0)
+
+    total_ref[...] = jnp.zeros_like(total_ref)
+    if ctx_n == 1:
+        attend(0)
+    else:
+        for peer, step, rows_copy, seg_copy in copies:
+            @pl.when(from_earlier(step))
+            def _(step=step, rows_copy=rows_copy, seg_copy=seg_copy):
+                rows_copy.wait_recv()
+                seg_copy.wait_recv()
+                block = lax.rem(ctx - step + ctx_n, ctx_n)
+                project(x_all[block], block, 1)
+
+        @pl.when(ctx == 0)
+        def _():
+            if ctx_n == 2:
+                attend(0)
+            else:
+                attend(ctx_n - 1)
+
+        @pl.when(ctx > 0)
+        def _():
+            attend(ctx_n - 1)
+
+        for peer, step, rows_copy, seg_copy in copies:
+            @pl.when(to_later(peer))
+            def _(rows_copy=rows_copy, seg_copy=seg_copy):
+                seg_copy.wait_send()
+                rows_copy.wait_send()
+
+    rank_out = nt(flat_ref[...], down).astype(BF)
+    rank_out_ref[...] = rank_out
+    part = jnp.where(column == 3, ADAPT_SCALE * rank_out.astype(F32), 0.0).astype(BF)
+
+    def out_chunk(i, carry):
+        cols = pl.ds(pl.multiple_of(i * 256, 256), 256)
+        mid_ref[:, cols] = (
+            x_ref[:, cols].astype(F32)
+            + nn(flat_ref[...], w_out_ref[:, cols])
+            + nn(part, up_ref[adapter, :, cols])
+        )
+        return carry
+
+    lax.fori_loop(0, model // 256, out_chunk, 0)
+    gain_two = gain_two_ref[...].astype(F32)
+    step_rows = 128
+
+    def norm_rows(i, carry):
+        rows = pl.ds(pl.multiple_of(i * step_rows, step_rows), step_rows)
+        mid = mid_ref[rows]
+        inv = lax.rsqrt(jnp.mean(mid * mid, -1, keepdims=True) + EPSILON)
+        rows_ref[rows] = (mid * inv * gain_two).astype(BF)
+        return carry
+
+    lax.fori_loop(0, tok // step_rows, norm_rows, 0)
+    logits_ref[...] = nt(rows_ref[...], router_ref[...]) + mixed_ref[...]
+
+
+def attention_forward(hidden, segments, mixed, ids, gain_one, w_qkv, w_out, down, up, gain_two, router):
+    ctx_n, exp_n = lax.axis_size("context"), lax.axis_size("expert")
+    tok, model = hidden.shape
+    pairs = model // 128
+    wide = down.shape[1]
+    cos_table, sin_table = rope_tables(ctx_n * tok, 64)
+    vmem = pl.BlockSpec(memory_space=pltpu.VMEM)
+    dma = pltpu.SemaphoreType.DMA
+    many = max(ctx_n - 1, 1)
+    shape = jax.ShapeDtypeStruct
+    return pl.pallas_call(
+        functools.partial(attention_kernel, (ctx_n, exp_n, wide // 4)),
+        out_shape=(
+            shape((pairs, tok, 128), BF),
+            shape((ctx_n, pairs, tok, 128), BF),
+            shape((ctx_n, pairs, tok, 128), BF),
+            shape((ctx_n, tok, model), BF),
+            shape((ctx_n, tok, wide), BF),
+            shape((tok, 128), F32),
+            shape((tok, model), BF),
+            shape((tok, wide), BF),
+            shape((tok, model), F32),
+            shape((tok, model), BF),
+            shape((tok, 128), F32),
+            shape((ctx_n, 8, tok), jnp.int32),
+        ),
+        in_specs=[pl.BlockSpec(memory_space=pltpu.SMEM)] + [vmem] * 12,
+        out_specs=(vmem,) * 12,
+        scratch_shapes=[
+            pltpu.VMEM((ctx_n, tok, model), BF),
+            pltpu.VMEM((ctx_n, tok, tok), F32),
+            dma((many,)), dma((many,)), dma((many,)), dma((many,)),
+        ],
+        compiler_params=pltpu.CompilerParams(
+            collective_id=2, has_side_effects=True, vmem_limit_bytes=VLIMIT
+        ),
+        name="attention_forward",
+    )(
+        ids, hidden, segments, mixed, gain_one.reshape(1, model), w_qkv, w_out, down, up,
+        gain_two.reshape(1, model), router, jnp.asarray(cos_table), jnp.asarray(sin_table),
+    )
+
+
+def put_tiles(tiles_ref, first, value):
+    for col in range(value.shape[1] // 128):
+        tiles_ref[first + col] = value[:, col * 128 : col * 128 + 128].astype(tiles_ref.dtype)
+
+
+def backward_kernel(
+    sizes, ids_ref, d_mid_ref, q_ref, k_ref, v_ref, normed_ref, rank_ref, total_ref, flat_ref,
+    rank_out_ref, x_ref, seg_all, gain_one_ref, w_qkv_ref, w_out_ref, down_ref, up_ref, cos_ref,
+    sin_ref,
+    grad_ref, tiles_ref, *scratch,
+):
+    ctx_n, exp_n, rank = sizes
+    (
+        recv_buf, do_ref, bias_ref, dk_acc, dv_acc, dq_all, dkv_all, send_buf, grad_up, grad_down,
+        normed_buf, send_sem, recv_sem, load_sem,
+    ) = scratch
+    ctx = lax.axis_index("context")
+    sequence = lax.axis_index("dp") * exp_n + lax.axis_index("expert")
+    tok, model = x_ref.shape
+    pairs, head_dim = model // 128, 64
+    entered = greet([("context", ctx_n)])
+    order = [ctx] + blocks_of(ctx_n, ctx, ctx_n - 1)
+
+    def fetch(j):
+        return pltpu.make_async_copy(
+            normed_ref.at[order[j]], normed_buf.at[min(j, 1)], load_sem.at[min(j, 1)]
+        )
+
+    fetch(0).start()
+    if ctx_n > 1:
+        fetch(1).start()
+    adapter = ids_ref[sequence]
+    down = down_ref[adapter]
+    up = up_ref[adapter]
+    wide = down.shape[0]
+    column = lax.broadcasted_iota(jnp.int32, (tok, wide), 1) // rank
+    d_branch = d_mid_ref[...].astype(BF)
+    d_rank_out = jnp.where(column == 3, ADAPT_SCALE * nt(d_branch, up), 0.0).astype(BF)
+    twice_out = jnp.where(column == 3, ADAPT_SCALE * rank_out_ref[...].astype(F32), 0.0).astype(BF)
+    grad_up[...] = tn(twice_out, d_branch)
+    grad_down[...] = tn(d_rank_out, flat_ref[...])
+
+    def attn_chunk(i, carry):
+        rows = pl.ds(pl.multiple_of(i * 256, 256), 256)
+        d_attn = nt(d_branch, w_out_ref[rows, :]) + nn(d_rank_out, down_ref[adapter, :, rows])
+        do_ref[2 * i] = d_attn[:, :128].astype(BF)
+        do_ref[2 * i + 1] = d_attn[:, 128:].astype(BF)
+        return carry
+
+    lax.fori_loop(0, model // 256, attn_chunk, 0)
+    lane = lax.broadcasted_iota(jnp.int32, (1, 128), 1)
+    marks = [(lane < 64), (lane >= 64)]
+    half_rows = tok // 2
+
+    def attend(count):
+        fill_bias(bias_ref, seg_all, ctx_n, ctx, tok, count)
+        others = blocks_of(ctx_n, ctx, count)
+
+        def pair(i, carry):
+            cols = pl.ds(pl.multiple_of(i * 128, 128), 128)
+            for half in (1, 0):
+                rows = slice(half * half_rows, (half + 1) * half_rows)
+                own_width = (half + 1) * half_rows
+                q = q_ref[i, rows]
+                d_out = do_ref[i, rows]
+                stats = total_ref[rows]
+                d_query = jnp.zeros((half_rows, 128), F32)
+                for head in range(2):
+                    mark = marks[head]
+                    q_head = jnp.where(mark, q, 0)
+                    do_head = jnp.where(mark, d_out, 0)
+                    total = jnp.sum(
+                        jnp.where(lane == 2 * i + head, stats, 0.0), -1, keepdims=True
+                    )
+                    parts = []
+                    delta = jnp.zeros((half_rows, 1), F32)
+                    for j, block in enumerate([ctx] + others):
+                        width = own_width if j == 0 else tok
+                        probs = jnp.exp(
+                            nt(q_head, k_ref[block, i, 0:width])
+                            + bias_ref[j, rows, 0:width]
+                            - total
+                        )
+                        d_probs = nt(do_head, v_ref[block, i, 0:width])
+                        delta = delta + jnp.sum(probs * d_probs, -1, keepdims=True)
+                        parts.append((probs, d_probs))
+                    for j, block in enumerate([ctx] + others):
+                        width = own_width if j == 0 else tok
+                        probs, d_probs = parts[j]
+                        d_scores = (probs * (d_probs - delta)).astype(BF)
+                        k_head = jnp.where(mark, k_ref[block, i, 0:width], 0)
+                        d_query = d_query + nn(d_scores, k_head)
+                        d_key = tn(q_head, d_scores)
+                        d_value = tn(do_head, probs.astype(BF))
+                        if half == 1 and head == 0:
+                            dk_acc[j, :, 0:width] = d_key
+                            dv_acc[j, :, 0:width] = d_value
+                        else:
+                            dk_acc[j, :, 0:width] += d_key
+                            dv_acc[j, :, 0:width] += d_value
+                start = pl.multiple_of(ctx * tok + half * half_rows, half_rows)
+                d_query = d_query * head_dim ** (-0.5)
+                dq_all[rows, cols] = turn(
+                    d_query, cos_ref[pl.ds(start, half_rows)], -sin_ref[pl.ds(start, half_rows)], head_dim
+                ).astype(BF)
+            for j, block in enumerate([ctx] + others):
+                start = pl.multiple_of(block * tok, tok)
+                d_key = turn(
+                    jnp.transpose(dk_acc[j]), cos_ref[pl.ds(start, tok)], -sin_ref[pl.ds(start, tok)], head_dim
+                )
+                dkv_all[j, 0, :, cols] = d_key.astype(BF)
+                dkv_all[j, 1, :, cols] = jnp.transpose(dv_acc[j]).astype(BF)
+            return carry
+
+        lax.fori_loop(0, pairs, pair, 0)
+
+    def fold(j, block, first, write):
+        normed = normed_buf[min(j, 1)]
+        ranks = rank_ref[block].astype(F32)
+        d_ranks = jnp.zeros((tok, wide), F32)
+        for p in range(first, 3):
+            d_proj = dq_all[...] if p == 0 else dkv_all[j, p - 1]
+            twice = jnp.where(column == p, ADAPT_SCALE * ranks, 0.0).astype(BF)
+            grad_up[...] += tn(twice, d_proj)
+            d_ranks = d_ranks + jnp.where(column == p, ADAPT_SCALE * nt(d_proj, up), 0.0)
+        d_ranks = d_ranks.astype(BF)
+        grad_down[...] += tn(d_ranks, normed)
+
+        def chunk(i, carry):
+            rows = pl.ds(pl.multiple_of(i * 256, 256), 256)
+            value = nn(d_ranks, down_ref[adapter, :, rows])
+            for p in range(first, 3):
+                d_proj = dq_all[...] if p == 0 else dkv_all[j, p - 1]
+                value = value + nt(d_proj, w_qkv_ref[rows, p * model : (p + 1) * model])
+            write(rows, value)
+            return carry
+
+        lax.fori_loop(0, model // 256, chunk, 0)
+
+    def write_own(cols, value):
+        grad_ref[:, cols] = value
+
+    copies = []
+    for step in range(1, ctx_n):
+        peer = lax.rem(ctx + step, ctx_n)
+        copies.append(
+            remote(send_buf, recv_buf.at[step - 1], send_sem.at[step - 1], recv_sem.at[step - 1], "context", peer)
+        )
+
+    if ctx_n == 1:
+        attend(0)
+    elif ctx_n == 2:
+        entered()
+
+        @pl.when(ctx == 0)
+        def _():
+            attend(0)
+    else:
+        entered()
+
+    def spread():
+        attend(ctx_n - 1)
+        for j, block in enumerate(blocks_of(ctx_n, ctx, ctx_n - 1)):
+            def write(cols, value):
+                send_buf[:, cols] = value.astype(BF)
+
+            fetch(j + 1).wait()
+            if j > 0:
+                copies[j - 1].wait_send()
+            fold(j + 1, block, 1, write)
+            copies[j].start()
+            if j + 2 < ctx_n:
+                fetch(j + 2).start()
+
+    if ctx_n == 2:
+        pl.when(ctx == 1)(spread)
+        pl.when(ctx == 0)(fetch(1).wait)
+    elif ctx_n > 2:
+        spread()
+    fetch(0).wait()
+    fold(0, ctx, 0, write_own)
+    if ctx_n == 2:
+        @pl.when(ctx == 0)
+        def _():
+            copies[0].wait_recv()
+
+        @pl.when(ctx == 1)
+        def _():
+            recv_buf[...] = jnp.zeros_like(recv_buf)
+    elif ctx_n > 2:
+        copies[-1].wait_send()
+        for step, item in enumerate(copies):
+            item.wait_recv()
+            load = pltpu.make_async_copy(recv_buf.at[step], send_buf, load_sem.at[0])
+            load.start()
+            load.wait()
+            grad_ref[...] += send_buf[...].astype(F32)
+    gain_one = gain_one_ref[...].astype(F32)
+
+    def finish(i, carry):
+        rows = pl.ds(pl.multiple_of(i * 128, 128), 128)
+        value = grad_ref[rows]
+        if ctx_n == 2:
+            value = value + recv_buf[0, rows].astype(F32)
+        x = x_ref[rows].astype(F32)
+        inv = lax.rsqrt(jnp.mean(x * x, -1, keepdims=True) + EPSILON)
+        scaled = value * gain_one
+        grad_ref[rows] = (
+            d_mid_ref[rows]
+            + inv * scaled
+            - x * (inv * inv * inv) * jnp.mean(scaled * x, -1, keepdims=True)
+        )
+        return carry
+
+    lax.fori_loop(0, tok // 128, finish, 0)
+    per = model // 128
+    for p in range(4):
+        put_tiles(tiles_ref, p * per, grad_down[p * rank : (p + 1) * rank])
+        put_tiles(tiles_ref, (4 + p) * per, grad_up[p * rank : (p + 1) * rank])
+    if ctx_n == 2:
+        @pl.when(ctx == 1)
+        def _():
+            copies[0].wait_send()
+
+
+def attention_backward(d_mid, saved, hidden, ids, gain_one, w_qkv, w_out, down, up):
+    ctx_n, exp_n = lax.axis_size("context"), lax.axis_size("expert")
+    tok, model = hidden.shape
+    pairs = model // 128
+    wide = down.shape[1]
+    cos_table, sin_table = rope_tables(ctx_n * tok, 64)
+    vmem = pl.BlockSpec(memory_space=pltpu.VMEM)
+    dma = pltpu.SemaphoreType.DMA
+    many = max(ctx_n - 1, 1)
+    shape = jax.ShapeDtypeStruct
+    q, k, v, normed, ranks, totals, flat, rank_out, seg_all = saved
+    in_specs = [vmem] * 18
+    in_specs[4] = pl.BlockSpec(memory_space=pl.ANY)
+    spill = ctx_n > 2
+    landing = ((many, tok, model), BF)
+    results = pl.pallas_call(
+        functools.partial(backward_kernel, (ctx_n, exp_n, wide // 4)),
+        out_shape=(shape((tok, model), F32), shape((8 * pairs, 16, 128), BF))
+        + ((shape(*landing),) if spill else ()),
+        in_specs=[pl.BlockSpec(memory_space=pltpu.SMEM)] + in_specs,
+        out_specs=(vmem,) * 2 + ((pl.BlockSpec(memory_space=pl.ANY),) if spill else ()),
+        scratch_shapes=([] if spill else [pltpu.VMEM(*landing)])
+        + [
+            pltpu.VMEM((pairs, tok, 128), BF),
+            pltpu.VMEM((ctx_n, tok, tok), BF if spill else F32),
+            pltpu.VMEM((ctx_n, 128, tok), F32),
+            pltpu.VMEM((ctx_n, 128, tok), F32),
+            pltpu.VMEM((tok, model), BF),
+            pltpu.VMEM((ctx_n, 2, tok, model), BF),
+            pltpu.VMEM((tok, model), BF),
+            pltpu.VMEM((wide, model), F32),
+            pltpu.VMEM((wide, model), F32),
+            pltpu.VMEM((min(ctx_n, 2), tok, model), BF),
+            dma((many,)), dma((many,)), dma((2,)),
+        ],
+        compiler_params=pltpu.CompilerParams(
+            collective_id=3, has_side_effects=True, vmem_limit_bytes=VLIMIT + 5 * 2**19
+        ),
+        name="attention_backward",
+    )(
+        ids, d_mid, q, k, v, normed, ranks, totals, flat, rank_out, hidden, seg_all,
+        gain_one.reshape(1, model), w_qkv, w_out, down, up, jnp.asarray(cos_table),
+        jnp.asarray(sin_table),
+    )
+    return results[:2]
 
 
 def to_tiles(table):
@@ -322,13 +832,12 @@
                 tile += 1
 
 
-def reduce_adapters(adapter_ids, expert_grads, attn_down, attn_up, adapters):
+def reduce_adapters(adapter_ids, expert_grads, attn, attn_shape, adapters):
     ctx_n, dp_n, exp_n = (lax.axis_size(axis) for axis in ("context", "dp", "expert"))
     experts = expert_grads[0].shape[1]
     packed = jnp.concatenate(
         [to_tiles(g)[:, e] for e in range(experts) for g in expert_grads], 1
     ).astype(BF)
-    attn = jnp.concatenate([to_tiles(attn_down), to_tiles(attn_up)], 0).astype(BF)
     tiles, attn_tiles = packed.shape[1], attn.shape[0]
     own_attn = attn_tiles // exp_n
     z_tiles = pl.cdiv(tiles + own_attn, ctx_n * dp_n)
@@ -363,8 +872,8 @@
         name="reduce_adapters",
     )(adapter_ids, packed, attn)
     shapes = [
-        (adapters,) + attn_down.shape,
-        (adapters,) + attn_up.shape,
+        (adapters,) + attn_shape,
+        (adapters,) + attn_shape,
     ] + [(adapters,) + g.shape[1:] for g in expert_grads]
     return pl.pallas_call(
         functools.partial(unpack_kernel, (x_tiles, z_tiles, own_attn)),
@@ -428,89 +937,32 @@
     rope_pos = tok_pos.astype(jnp.float32)
     seg_local = segment_ids[0]
     head_shape = (tok_count, HEADS, model_dim // HEADS)
-    resid_in = hidden_in[0].astype(jnp.float32)
-    gain_one = attn_gain.astype(jnp.float32)
-    inv_one = lax.rsqrt(jnp.mean(resid_in * resid_in, -1, keepdims=True) + EPSILON)
-    normed_low = (resid_in * inv_one * gain_one).astype(jnp.bfloat16)
-    down_sel = lax.dynamic_index_in_dim(attn_down, my_adapter, 0, keepdims=False)
-    up_sel = lax.dynamic_index_in_dim(attn_up, my_adapter, 0, keepdims=False)
-    rank_qkv = bdot("td,pdr->ptr", normed_low, down_sel[:3]).astype(jnp.bfloat16)
-    proj_qkv = bdot("td,de->te", normed_low, w_qkv).reshape(
-        tok_count, 3, model_dim
-    ) + ADAPT_SCALE * bdot("ptr,prd->tpd", rank_qkv, up_sel[:3])
-    queries = rotate(proj_qkv[:, 0].reshape(head_shape), rope_pos, 1.0).astype(jnp.bfloat16)
-    key_rows = rotate(proj_qkv[:, 1].reshape(head_shape), rope_pos, 1.0).astype(jnp.bfloat16)
-    value_rows = proj_qkv[:, 2].reshape(head_shape).astype(jnp.bfloat16)
-    all_keys, all_values, all_segs = (
-        lax.all_gather(key_rows, "context", axis=0, tiled=True),
-        lax.all_gather(value_rows, "context", axis=0, tiled=True),
-        lax.all_gather(seg_local, "context", axis=0, tiled=True),
-    )
-    block_total = seq_total // key_block
-
-    def key_slice(block_index):
-        offset = block_index * key_block
-        return (
-            lax.dynamic_slice_in_dim(all_keys, offset, key_block, 0),
-            lax.dynamic_slice_in_dim(all_values, offset, key_block, 0),
-            lax.dynamic_slice_in_dim(all_segs, offset, key_block, 0),
-            offset + jnp.arange(key_block, dtype=jnp.int32),
-        )
-
-    def max_step(block_index, totals):
-        run_max, run_sum = totals
-        blk_keys, blk_values, blk_segs, blk_pos = key_slice(block_index)
-        scores = masked_scores(queries, blk_keys, tok_pos, seg_local, blk_pos, blk_segs)
-        new_max = jnp.maximum(run_max, jnp.max(scores, -1))
-        new_sum = run_sum * jnp.exp(run_max - new_max) + jnp.sum(
-            jnp.exp(scores - new_max[:, :, None]), -1
-        )
-        return (new_max, new_sum)
-
-    start_max = jnp.full((HEADS, tok_count), NEG, jnp.float32)
-    run_max, run_sum = lax.fori_loop(
-        0, block_total, max_step, (start_max, jnp.zeros((HEADS, tok_count), jnp.float32))
-    )
-    log_total = run_max + jnp.log(run_sum)
-
-    def value_step(block_index, totals):
-        high_acc, low_acc = totals
-        blk_keys, blk_values, blk_segs, blk_pos = key_slice(block_index)
-        probs_block = jnp.exp(
-            masked_scores(queries, blk_keys, tok_pos, seg_local, blk_pos, blk_segs)
-            - log_total[:, :, None]
-        )
-        rounded = probs_block.astype(jnp.bfloat16)
-        residue = (probs_block - rounded.astype(jnp.float32)).astype(jnp.bfloat16)
-        return (
-            high_acc + bdot("hqk,khd->qhd", rounded, blk_values),
-            low_acc + bdot("hqk,khd->qhd", residue, blk_values),
-        )
-
-    zero_heads = jnp.zeros(head_shape, jnp.float32)
-    attn_high, attn_low = lax.fori_loop(0, block_total, value_step, (zero_heads, zero_heads))
-    attn_exact = attn_high + attn_low
-    attn_flat = attn_high.reshape(tok_count, model_dim).astype(jnp.bfloat16)
-    rank_out = bdot("td,dr->tr", attn_flat, down_sel[3]).astype(jnp.bfloat16)
-    mid_resid = (
-        resid_in
-        + bdot("td,de->te", attn_flat, w_out)
-        + ADAPT_SCALE * bdot("tr,rd->td", rank_out, up_sel[3])
+    rank_dim = attn_up.shape[2]
+    down_all = jnp.swapaxes(attn_down, 2, 3).reshape(adapter_count, 4 * rank_dim, model_dim)
+    up_all = attn_up.reshape(adapter_count, 4 * rank_dim, model_dim)
+    router_rows = jnp.concatenate(
+        [router_weight.T, const_mix.transpose(0, 2, 1).reshape(4, model_dim)], 0
+    )
+    router_rows = jnp.pad(router_rows, ((0, 128 - router_rows.shape[0]), (0, 0)))
+    mixed = jnp.pad(fdot("te,ef->tf", prev_logits[0], gate_mix), ((0, 0), (0, 128 - kind_count)))
+    (
+        q_pairs, k_pairs, v_pairs, normed_all, rank_all, log_cols, attn_flat, rank_out_all, mid_resid,
+        rows_low, logits_all, seg_all,
+    ) = attention_forward(
+        hidden_in[0], segment_ids, mixed, adapter_ids, attn_gain, w_qkv, w_out, down_all, up_all,
+        ffn_gain, router_rows,
     )
     gain_two = ffn_gain.astype(jnp.float32)
     inv_two = lax.rsqrt(jnp.mean(mid_resid * mid_resid, -1, keepdims=True) + EPSILON)
     normed_two = mid_resid * inv_two * gain_two
-    rows_low = normed_two.astype(jnp.bfloat16)
-    logits = bdot("td,de->te", rows_low, router_weight) + fdot(
-        "te,ef->tf", prev_logits[0], gate_mix
-    )
+    logits = logits_all[:, :kind_count]
     probs_all = jax.nn.softmax(logits, -1)
     route_tok = routes[0]
     kind_match = (
         route_tok[:, :, None] == jnp.arange(kind_count, dtype=jnp.int32)[None, None, :]
     ).astype(jnp.float32)
     gate_values = jnp.sum(kind_match * probs_all[:, None, :], -1)
-    mix_const = jax.nn.softmax(bdot("td,idc->tic", rows_low, const_mix), -1)
+    mix_const = jax.nn.softmax(logits_all[:, kind_count : kind_count + 4].reshape(tok_count, 2, 2), -1)
     const_full = const_vec.astype(jnp.float32)
     const_terms = (
         mix_const[:, :, 0:1] * normed_two[:, None, :]
@@ -608,79 +1060,18 @@
         * (inv_two * inv_two * inv_two)
         * jnp.mean(scaled_two * mid_resid, -1, keepdims=True)
     )
-    d_branch = d_mid.astype(jnp.bfloat16)
-    d_rank_out = (ADAPT_SCALE * bdot("td,rd->tr", d_branch, up_sel[3])).astype(jnp.bfloat16)
-    grad_up_out = ADAPT_SCALE * bdot("tr,td->rd", rank_out, d_branch)
-    grad_down_out = bdot("td,tr->rd", attn_flat, d_rank_out)
-    d_attn = (
-        (bdot("te,de->td", d_branch, w_out) + bdot("tr,dr->td", d_rank_out, down_sel[3]))
-        .astype(jnp.bfloat16)
-        .reshape(head_shape)
-    )
-    row_delta = jnp.transpose(jnp.sum(d_attn.astype(jnp.float32) * attn_exact, -1))
-
-    def grad_step(block_index, totals):
-        d_query_acc, d_key_all, d_value_all = totals
-        blk_keys, blk_values, blk_segs, blk_pos = key_slice(block_index)
-        d_query_part, d_key_part, d_value_part = block_grads(
-            queries,
-            d_attn,
-            log_total,
-            row_delta,
-            tok_pos,
-            seg_local,
-            blk_keys,
-            blk_values,
-            blk_pos,
-            blk_segs,
-        )
-        offset = block_index * key_block
-        return (
-            d_query_acc + d_query_part,
-            lax.dynamic_update_slice_in_dim(d_key_all, d_key_part, offset, 0),
-            lax.dynamic_update_slice_in_dim(d_value_all, d_value_part, offset, 0),
-        )
-
-    zero_all = jnp.zeros((seq_total,) + head_shape[1:], jnp.float32)
-    d_queries, d_key_all, d_value_all = lax.fori_loop(
-        0, block_total, grad_step, (zero_heads, zero_all, zero_all)
-    )
-    d_keys, d_values = (
-        lax.psum_scatter(
-            d_key_all.astype(jnp.bfloat16), "context", scatter_dimension=0, tiled=True
-        ).astype(jnp.float32),
-        lax.psum_scatter(
-            d_value_all.astype(jnp.bfloat16), "context", scatter_dimension=0, tiled=True
-        ).astype(jnp.float32),
-    )
-    d_query_flat = rotate(d_queries, rope_pos, -1.0).reshape(tok_count, model_dim)
-    d_key_flat = rotate(d_keys, rope_pos, -1.0).reshape(tok_count, model_dim)
-    d_proj = jnp.stack(
-        [d_query_flat, d_key_flat, d_values.reshape(tok_count, model_dim)], 1
-    ).astype(jnp.bfloat16)
-    d_rank_qkv = (ADAPT_SCALE * bdot("tpd,prd->ptr", d_proj, up_sel[:3])).astype(jnp.bfloat16)
-    grad_up_qkv = ADAPT_SCALE * bdot("ptr,tpd->prd", rank_qkv, d_proj)
-    grad_down_qkv = bdot("td,ptr->prd", normed_low, d_rank_qkv)
-    d_normed_one = bdot("te,de->td", d_proj.reshape(tok_count, 3 * model_dim), w_qkv) + bdot(
-        "ptr,pdr->td", d_rank_qkv, down_sel[:3]
-    )
-    scaled_one = d_normed_one * gain_one
-    grad_in = (
-        d_mid
-        + inv_one * scaled_one
-        - resid_in
-        * (inv_one * inv_one * inv_one)
-        * jnp.mean(scaled_one * resid_in, -1, keepdims=True)
-    )
-    grad_down_all = jnp.concatenate([grad_down_qkv, grad_down_out[None]], 0)
-    grad_up_all = jnp.concatenate([grad_up_qkv, grad_up_out[None]], 0)
+    grad_in, attn_tiles = attention_backward(
+        d_mid,
+        (q_pairs, k_pairs, v_pairs, normed_all, rank_all, log_cols, attn_flat, rank_out_all, seg_all),
+        hidden_in[0], adapter_ids, attn_gain, w_qkv, w_out, down_all, up_all,
+    )
     in_down, in_up, out_down, out_up = owner_grads
     sources, experts, _, rank_dim, ffn_width = in_up.shape
     sums = reduce_adapters(
         adapter_ids,
         (in_down, in_up.reshape(sources, experts, 2 * rank_dim, ffn_width), out_down, out_up),
-        grad_down_all.reshape(4 * rank_dim, model_dim),
-        grad_up_all.reshape(4 * rank_dim, model_dim),
+        attn_tiles,
+        (4 * rank_dim, model_dim),
         adapter_count,
     )
     grad_attn_down = jnp.swapaxes(sums[0].reshape(adapter_count, 4, rank_dim, model_dim), 2, 3)

time: 741 us -> 561 us (0.76)
  matrix products: 233 us -> 98.2 us
  Pallas kernels: 153 us -> 252 us
  waiting for transfers between devices: 68.2 us -> 20.9 us
  local copies, waits for them, and re-layouts: 156 us -> 114 us
  other arithmetic: 79.2 us -> 46 us
  between operations: 17.5 us -> 2.08 us
    dot_general x58 -> x23, matrix products: 227 us -> 89.7 us  [bdot(): return jnp.einsum(form, left, right, preferred_element_type=jnp.float32)]
    pallas_call x0 -> x2, Pallas kernels: none -> 99.4 us  [the longest x1 72.4 us: attention_backward(): pl.pallas_call(functools.partial(backward_kernel, (ctx_n, exp_n, wide //...]
    reduce_scatter x2 -> x0, waiting for transfers between devices: 30.6 us -> none  [the longest x1 27.5 us: local(): lax.psum_scatter(d_key_all.astype(jnp.bfloat16), 'context', scatter_dimen...]
    reduce_sum x4 -> x1, other arithmetic: 16.9 us -> 0.18 us  [local(): jnp.mean(mid_resid * mid_resid, -1, keepdims=True) + EPSILON]
    while x46 -> x0, local copies, waits for them, and re-layouts: 13 us -> none
    slice x6 -> x3, local copies, waits for them, and re-layouts: 13 us -> 0.52 us  [the longest x2 5.06 us: local(): proj_qkv[:, 0].reshape(head_shape)]
    all_to_all x1, waiting for transfers between devices: 19.3 us -> 7.42 us  [local(): lax.all_to_all(d_outgoing, 'expert', split_axis=0, concat_axis=0, tiled=T...]
    all_to_all x1, waiting for transfers between devices: 10.4 us -> 0.01 us  [local(): lax.all_to_all(outgoing, 'expert', split_axis=0, concat_axis=0, tiled=True)]
  transfers between devices with their start and end apart: 8 -> 4, of which waited for: 5 -> 2; matrix products, arithmetic and copies ran while one was open for 18% -> 14% of each run, Pallas kernels for 0% -> 0%
where the time goes in v2:
time: 561 us; the launch traced here: 553 us
  Pallas kernels  252 us (45%)
  local copies, waits for them, and re-layouts  114 us (20%)
  matrix products  98.2 us (18%)
  other arithmetic  46 us (8%)
  waiting for transfers between devices  20.9 us (4%)
  starting transfers between devices  19.9 us (4%)
    pallas_call x1, Pallas kernels, reduce_adapters(): pl.pallas_call(functools.partial(reduce_kernel, sizes), out_shape=(jax.Sh...  144 us
    dot_general x23, matrix products, bdot(): return jnp.einsum(form, left, right, preferred_element_type=jnp.float32)  89.7 us
    pallas_call x1, Pallas kernels, attention_backward(): pl.pallas_call(functools.partial(backward_kernel, (ctx_n, exp_n, wide //...  72.4 us
    pallas_call x1, Pallas kernels, attention_forward(): pl.pallas_call(functools.partial(attention_kernel, (ctx_n, exp_n, wide //...  27 us
    broadcast_in_dim x6, local copies, waits for them, and re-layouts, local(): jnp.where((route_tok == ffn_count + 2 + const_index)[:, :, None], const_t...  20.2 us
    unnamed x186, local copies, waits for them, and re-layouts  15.5 us
    reduce_sum x1, other arithmetic, local(): d_normed = d_normed + jnp.sum(d_back_rows, 1)  14.5 us
    all_to_all x1, waiting for transfers between devices, local(): lax.all_to_all(d_kept.astype(jnp.bfloat16), 'expert', split_axis=0, conca...  13.5 us
  transfers between devices with their start and end apart: 4, of which 2 were waited for; matrix products, arithmetic and copies ran while one was open for 14% of the time, Pallas kernels for 0%

profile of v2, /device:TPU:25, one launch (start us, length us, event | category | flops | bytes accessed | tf_op | source)
XLA Modules:
  0.0 553.0 jit_solution(6366241731969374930)
XLA Ops:
  10.0 27.0 %attention_forward.1 = (bf16[6,512,128]{2,1,0:T(8,128)(2,1)}, bf16[2,6,512,128]{3,2,1,0:T(8,128)(2,1)}, bf16[2,6,512,128]{3,2,1,0:T(8,128)(2,1)}, bf16[2,512,768...) custom-call(s32[16]{0:T(128)} %ids_ref.5, ...), custom_call_target="tpu_custom_call" | custom-call | tf_op jit(solution)/shard_map/attention_forward/pallas_call | solution.py:355
  37.0 1.9 broadcast_in_dim.144
  40.5 2.3 reduce-window.6
  44.7 7.0 %scatter_custom_fusion = bf16[1024,768]{1,0:T(8,128)(2,1)} fusion(s32[1024]{0:T(1024)S(1)} %bitcast.275, bf16[1024,768]{1,0:T(8,128)(2,1)} %reshape.454, bf16[]{:T(256)} %constant.22.clone.1), kind=kCustom, calls=%fused_computation.108 | custom fusion | bytes 1573376 | tf_op jit(solution)/shard_map/scatter | solution.py:983
  51.7 6.0 %all-to-all-start = ((bf16[4,2,128,768]{3,2,1,0:T(8,128)(2,1)}), bf16[4,2,128,768]{3,2,1,0:T(8,128)(2,1)}, u32[]{:S(2)}, u32[]{:S(2)}) async-start(bf16[4,2,128,768]{3,2,1,0:T(8,128)(2,1)} %bitcast.10), calls=%async_computation | async-start | bytes 3145728 | tf_op jit(solution)/shard_map/all_to_all | solution.py:995
  57.8 2.6 convolution_convert_fusion.3
  60.5 1.6 convolution_convert_fusion.1
  66.0 2.6 multiply_add_fusion
  68.6 2.4 fusion.155
  73.6 4.1 broadcast_in_dim.151
  77.7 5.3 broadcast_in_dim.164
  83.0 2.7 broadcast_in_dim.154
  85.7 5.6 %broadcast_in_dim.167 = f32[1024,768]{1,0:T(8,128)} reshape(f32[512,2,768]{2,1,0:T(2,128)} %broadcast_in_dim.154) | data formatting | bytes 6291456 | tf_op jit(solution)/shard_map/jit(_where)/broadcast_in_dim | solution.py:1005
  91.4 2.7 broadcast_in_dim.147
  94.1 5.3 broadcast_in_dim.160
  103.1 2.4 convolution_convert_fusion.5
  105.5 15.1 %fusion.5 = f32[4,2,128,4096]{3,2,0,1:T(8,128)} fusion(bf16[2,768,4096]{2,1,0:T(8,128)(2,1)} %param.41, bf16[4,2,128,768]{3,2,1,0:T(8,128)(2,1)} %all-to-all-done), kind=kOutput, calls=%fused_computation.11 | convolution fusion | flops 6442450944 | bytes 30932992 | tf_op jit(solution)/shard_map/jecd,edf->jecf/dot_general | solution.py:27
  120.6 4.8 slice_add_fusion.1
  125.4 10.5 %multiply_convert_fusion = (bf16[4,2,128,2048]{3,2,0,1:T(8,128)(2,1)S(1)}, f32[4,2,128,2048]{3,2,0,1:T(8,128)}) fusion(f32[4,2,128,2048]{3,2,0,1:T(8,128)S(1)} %slice_add_fusion.1, bf16[4,2,16,2048]{3,0,2,1:T(4,128)(2,1)S(1)} %get-tuple-element.120, bf16[4,2,128,16]{2,3,1,0:T(8,128)(2,1)S(1)} %get-tuple-element.122, f32[4,2,128,4096]{3,2,0,1:T(8,128)} %fusion.5), kind=kOutput, calls=%fused_computation.23 | convolution fusion | flops 83886080 | bytes 29917184 | tf_op jit(solution)/shard_map/jecr,jerf->jecf/dot_general | solution.py:27
  137.9 6.2 %fusion.34 = bf16[4,2,128,768]{3,2,0,1:T(8,128)(2,1)S(1)} fusion(f32[4,2,128,768]{3,2,0,1:T(8,128)S(1)} %fusion.102, bf16[4,2,128,2048]{3,2,0,1:T(8,128)(2,1)S(1)} %get-tuple-element.137, bf16[2,2048,768]{2,1,0:T(8,128)(2,1)} %param.42), kind=kOutput, calls=%fused_computation.45 | convolution fusion | flops 3223584768 | bytes 15204352 | tf_op jit(solution)/shard_map/jecf,efd->jecd/dot_general | solution.py:27
  145.3 3.9 all-to-all-start.1
  158.6 2.7 mul.364
  161.3 5.3 mul.365
  168.7 5.2 gather_fusion
  173.9 4.6 gather.11
  178.5 5.0 multiply_reduce_fusion
  187.6 7.0 %scatter_custom_fusion.1 = bf16[1024,768]{1,0:T(8,128)(2,1)} fusion(s32[1024]{0:T(1024)} %bitcast.276, f32[1024,768]{1,0:T(8,128)S(1)} %copy-done.5, f32[1024]{0:T(1024)S(1)} %mul.400, bf16[]{:T(256)} %constant.22.clone.1), kind=kCustom, calls=%fused_computation.58 | custom fusion | flops 1572864 | bytes 4723200 | tf_op jit(solution)/shard_map/scatter | solution.py:1043
  194.6 4.5 all-to-all-start.2
  204.0 2.3 fusion.57
  206.9 2.0 fusion.124
  208.9 1.9 fusion.107
  210.9 7.4 %all-to-all-done.2 = bf16[4,2,128,768]{3,2,1,0:T(8,128)(2,1)S(1)} async-done(((bf16[4,2,128,768]{3,2,1,0:T(8,128)(2,1)}), bf16[4,2,128,768]{3,2,1,0:T(8,128)(2,1)S(1)}, u32[]{:S(2)}, u32[]{:S(2)}) %all-to-all-start.2) | async-done | bytes 1572896 | tf_op jit(solution)/shard_map/all_to_all | solution.py:1046
  218.3 8.5 %fusion.17 = f32[2,4,128,2048]{3,2,1,0:T(8,128)} fusion(bf16[2,2048,768]{2,1,0:T(8,128)(2,1)} %param.42, bf16[4,2,128,768]{3,2,1,0:T(8,128)(2,1)S(1)} %all-to-all-done.2), kind=kOutput, calls=%fused_computation.26 | convolution fusion | flops 3221225472 | bytes 16252928 | tf_op jit(solution)/shard_map/jecd,efd->jecf/dot_general | solution.py:27
  227.3 11.1 %fusion.10 = (bf16[4,2,128,2048]{3,2,0,1:T(8,128)(2,1)S(1)}, bf16[4,2,128,2048]{3,2,0,1:T(8,128)(2,1)S(1)}) fusion(f32[4,2,128,2048]{3,2,0,1:T(8,128)} %get-tuple-element.138, f32[4,2,128,2048]{3,2,0,1:T(8,128)} %copy-done.12, bf16[4,2,2048,16]{2,0,3,1:T(4,128)(2,1)S(1)} %copy-done.40, bf16[4,2,128,16]{2,3,1,0:T(8,128)(2,1)S(1)} %fusion.69, ...), kind=kOutput, calls=%fused_computation.14 | convolution fusion | flops 100663296 | bytes 34111488 | tf_op jit(solution)/shard_map/jecr,jefr->jecf/dot_general | solution.py:27
  247.5 2.3 fusion.91
  249.8 1.7 convolution_convert_fusion.2
  256.3 13.3 %fusion.33 = bf16[4,2,128,768]{3,2,0,1:T(8,128)(2,1)S(1)} fusion(f32[4,2,128,768]{3,2,0,1:T(8,128)} %fusion.91, bf16[2,768,4096]{2,1,0:T(8,128)(2,1)} %param.41, bf16[4,2,128,2048]{3,2,0,1:T(8,128)(2,1)} %copy-done.17, bf16[4,2,128,2048]{3,2,0,1:T(8,128)(2,1)} %copy-done.16), kind=kOutput, calls=%fused_computation.43 | convolution fusion | flops 6460801024 | bytes 25690112 | tf_op jit(solution)/shard_map/jecf,edf->jecd/dot_general | solution.py:27
  270.8 5.5 all-to-all-start.3
  282.0 13.5 %all-to-all-done.3 = bf16[4,2,128,768]{3,2,1,0:T(8,128)(2,1)} async-done(((bf16[4,2,128,768]{3,2,1,0:T(8,128)(2,1)}), bf16[4,2,128,768]{3,2,1,0:T(8,128)(2,1)}, u32[]{:S(2)}, u32[]{:S(2)}) %all-to-all-start.3) | async-done | bytes 1572896 | tf_op jit(solution)/shard_map/all_to_all | solution.py:1048
  295.6 1.6 bitcast_convert_fusion
  297.2 5.2 gather_fusion.1
  302.5 5.3 gather.13
  307.9 14.5 %select_reduce_fusion = (f32[512,768]{1,0:T(8,128)S(1)}, f32[512,768]{1,0:T(8,128)S(1)}) fusion(f32[512,2,768]{2,1,0:T(2,128)} %gather.13, pred[512,2]{1,0:T(8,128)(4,1)} %copy.248, f32[512,768]{1,0:T(8,128)S(1)} %copy-done.9, pred[512,2]{1,0:T(8,128)(4,1)} %copy.273, f32[512,768]{1,0:T(8,128)} %get-tuple-element.142, pred[512,2]{1,0:T(8,128)(4,1)S(1)} %copy-done.38, ...), kind=kLoop, calls=%fused_computation.46 | loop fusion | flops 8650752 | bytes 12591104 | tf_op jit(solution)/shard_map/reduce_sum | solution.py:1054
  322.6 2.0 multiply_reduce_fusion.2
  324.6 1.9 fusion.64
  326.5 72.4 %attention_backward.1 = (f32[512,768]{1,0:T(8,128)}, bf16[48,16,128]{2,1,0:T(8,128)(2,1)}) custom-call(s32[16]{0:T(128)} %ids_ref.5, f32[512,768]{1,0:T(8,128)} %get-tuple-element.117.d_mid_ref, bf16[6,512,128]{2,1,0:T(8,128)(2,1)} %get-tuple-element.34.q_ref, bf16[2,6,512,128]{3,2,1,0:T(8,128)(2,1)} %get-tuple-element.35.k_ref, ...), custom_call_target="tpu_custom_call" | custom-call | tf_op jit(solution)/shard_map/attention_backward/pallas_call | solution.py:628
  398.9 144.0 %reduce_adapters.1 = (bf16[2,4,8,18,16,128]{5,4,3,2,1,0:T(8,128)(2,1)}, bf16[4,12,8,16,128]{4,3,2,1,0:T(8,128)(2,1)}) custom-call(s32[16]{0:T(128)} %ids_ref.5, bf16[4,132,16,128]{3,2,1,0:T(8,128)(2,1)} %fusion.109.grads_ref, bf16[48,16,128]{2,1,0:T(8,128)(2,1)} %get-tuple-element.44.attn_ref), custom_call_target="tpu_custom_call" | custom-call | tf_op jit(solution)/shard_map/reduce_adapters/pallas_call | solution.py:848
  542.9 8.7 %unpack_adapters.1 = (f32[8,64,768]{2,1,0:T(8,128)}, f32[8,64,768]{2,1,0:T(8,128)}, f32[8,2,32,768]{3,2,1,0:T(8,128)}, f32[8,2,32,2048]{3,2,1,0:T(8,128)}, f32[8...) custom-call(bf16[2,4,8,18,16,128]{5,4,3,2,1,0:T(8,128)(2,1)} %get-tuple-element.45.table_ref, ...), custom_call_target="tpu_custom_call" | custom-call | tf_op jit(solution)/shard_map/unpack_adapters/pallas_call | solution.py:878
  (279 shorter events, 69.4 us)
Async XLA Ops:
  0.6 59.8 %copy-start = (bf16[8,2,2048,16]{2,3,1,0:T(8,128)(2,1)S(1)}, bf16[8,2,2048,16]{2,3,1,0:T(8,128)(2,1)}, u32[]{:S(2)}) copy-start(bf16[8,2,2048,16]{2,3,1,0:T(8,128)(2,1)} %param.45) | copy-start | bytes 3145732
  44.6 13.1 %copy-start.77 = (bf16[768]{0:T(1024)(128)(2,1)S(1)}, bf16[768]{0:T(1024)(128)(2,1)}, u32[]{:S(2)}) copy-start(bf16[768]{0:T(1024)(128)(2,1)} %param.36) | copy-start | bytes 4612
  44.7 13.1 %copy-start.79 = (s32[16]{0:T(128)S(1)}, s32[16]{0:T(128)}, u32[]{:S(2)}) copy-start(s32[16]{0:T(128)} %ids_ref.5) | copy-start | bytes 196
  51.7 51.4 %all-to-all-start = ((bf16[4,2,128,768]{3,2,1,0:T(8,128)(2,1)}), bf16[4,2,128,768]{3,2,1,0:T(8,128)(2,1)}, u32[]{:S(2)}, u32[]{:S(2)}) async-start(bf16[4,2,128,768]{3,2,1,0:T(8,128)(2,1)} %bitcast.10), calls=%async_computation | async-start | bytes 3145728 | tf_op jit(solution)/shard_map/all_to_all | solution.py:995
  65.2 26.2 %copy-start.6 = (f32[512,768]{1,0:T(8,128)}, f32[512,768]{1,0:T(8,128)S(1)}, u32[]{:S(2)}) copy-start(f32[512,768]{1,0:T(8,128)S(1)} %multiply_multiply_fusion) | copy-start | bytes 4718596
  72.4 10.6 %copy-start.8 = (f32[512,768]{1,0:T(8,128)}, f32[512,768]{1,0:T(8,128)S(1)}, u32[]{:S(2)}) copy-start(f32[512,768]{1,0:T(8,128)S(1)} %get-tuple-element.141) | copy-start | bytes 4718596
  103.1 17.5 %copy-start.25 = (bf16[4,2,16,2048]{3,0,2,1:T(4,128)(2,1)}, bf16[4,2,16,2048]{3,0,2,1:T(4,128)(2,1)S(1)}, u32[]{:S(2)}) copy-start(bf16[4,2,16,2048]{3,0,2,1:T(4,128)(2,1)S(1)} %get-tuple-element.119) | copy-start | bytes 1572868
  103.1 22.3 %copy-start.41 = (bf16[4,2,16,2048]{3,0,2,1:T(4,128)(2,1)}, bf16[4,2,16,2048]{3,0,2,1:T(4,128)(2,1)S(1)}, u32[]{:S(2)}) copy-start(bf16[4,2,16,2048]{3,0,2,1:T(4,128)(2,1)S(1)} %get-tuple-element.120) | copy-start | bytes 1572868
  105.5 15.1 %copy-start.44 = (bf16[4,2,128,32]{2,3,1,0:T(8,128)(2,1)}, bf16[4,2,128,32]{2,3,1,0:T(8,128)(2,1)S(1)}, u32[]{:S(2)}) copy-start(bf16[4,2,128,32]{2,3,1,0:T(8,128)(2,1)S(1)} %convolution_convert_fusion.5) | copy-start | bytes 196612
  125.3 10.5 %copy-start.12 = (f32[4,2,128,2048]{3,2,0,1:T(8,128)}, f32[4,2,128,2048]{3,2,0,1:T(8,128)S(1)}, u32[]{:S(2)}) copy-start(f32[4,2,128,2048]{3,2,0,1:T(8,128)S(1)} %slice_add_fusion.1) | copy-start | bytes 25165828
  125.4 10.5 %copy-start.39 = (bf16[4,2,2048,16]{2,0,3,1:T(4,128)(2,1)S(1)}, bf16[4,2,2048,16]{2,0,3,1:T(4,128)(2,1)}, u32[]{:S(2)}) copy-start(bf16[4,2,2048,16]{2,0,3,1:T(4,128)(2,1)} %convolution_convert_fusion.1) | copy-start | bytes 1572868
  145.3 23.3 %all-to-all-start.1 = ((bf16[4,2,128,768]{3,2,1,0:T(8,128)(2,1)}), bf16[4,2,128,768]{3,2,1,0:T(8,128)(2,1)S(1)}, u32[]{:S(2)}, u32[]{:S(2)}) async-start(bf16[4,2,128,768]{3,2,1,0:T(8,128)(2,1)} %copy.267), calls=%async_computation.1 | async-start | bytes 3145728 | tf_op jit(solution)/shard_map/all_to_all | solution.py:997
  150.0 11.3 %copy-start.35 = (pred[512,2]{1,0:T(8,128)(4,1)}, pred[512,2]{1,0:T(8,128)(4,1)S(1)}, u32[]{:S(2)}) copy-start(pred[512,2]{1,0:T(8,128)(4,1)S(1)} %copy.268) | copy-start | bytes 3076
  151.6 9.7 %copy-start.37 = (pred[512,2]{1,0:T(8,128)(4,1)}, pred[512,2]{1,0:T(8,128)(4,1)S(1)}, u32[]{:S(2)}) copy-start(pred[512,2]{1,0:T(8,128)(4,1)S(1)} %copy.269) | copy-start | bytes 3076
  161.3 7.3 %copy-start.72 = (s32[1024,1]{0,1:T(1,128)S(1)}, s32[1024,1]{0,1:T(1,128)}, u32[]{:S(2)}) copy-start(s32[1024,1]{0,1:T(1,128)} %get-tuple-element.123) | copy-start | bytes 12292
  168.6 9.9 %copy-start.80 = (pred[1024]{0:T(1024)(128)(4,1)S(1)}, pred[1024]{0:T(1024)(128)(4,1)}, u32[]{:S(2)}) copy-start(pred[1024]{0:T(1024)(128)(4,1)} %broadcast_in_dim.158) | copy-start | bytes 3076
  168.6 9.9 %copy-start.81 = (pred[1024]{0:T(1024)(128)(4,1)S(1)}, pred[1024]{0:T(1024)(128)(4,1)}, u32[]{:S(2)}) copy-start(pred[1024]{0:T(1024)(128)(4,1)} %broadcast_in_dim.162) | copy-start | bytes 3076
  168.6 9.9 %copy-start.82 = (pred[1024]{0:T(1024)(128)(4,1)S(1)}, pred[1024]{0:T(1024)(128)(4,1)}, u32[]{:S(2)}) copy-start(pred[1024]{0:T(1024)(128)(4,1)} %broadcast_in_dim.165) | copy-start | bytes 3076
  168.6 9.9 %copy-start.83 = (pred[1024]{0:T(1024)(128)(4,1)S(1)}, pred[1024]{0:T(1024)(128)(4,1)}, u32[]{:S(2)}) copy-start(pred[1024]{0:T(1024)(128)(4,1)} %broadcast_in_dim.156) | copy-start | bytes 3076
  194.5 8.8 %copy-start.61 = (pred[512,2]{0,1:T(4,128)(4,1)S(1)}, pred[512,2]{0,1:T(4,128)(4,1)}, u32[]{:S(2)}) copy-start(pred[512,2]{0,1:T(4,128)(4,1)} %copy-done.60) | copy-start | bytes 3076
  194.5 8.8 %copy-start.62 = (pred[512,2]{0,1:T(4,128)(4,1)S(1)}, pred[512,2]{0,1:T(4,128)(4,1)}, u32[]{:S(2)}) copy-start(pred[512,2]{0,1:T(4,128)(4,1)} %get-tuple-element.131) | copy-start | bytes 3076
  194.5 8.8 %copy-start.63 = (pred[512,2]{0,1:T(4,128)(4,1)S(1)}, pred[512,2]{0,1:T(4,128)(4,1)}, u32[]{:S(2)}) copy-start(pred[512,2]{0,1:T(4,128)(4,1)} %get-tuple-element.132) | copy-start | bytes 3076
  194.5 9.4 %copy-start.3 = (f32[512,768]{1,0:T(8,128)S(1)}, f32[512,768]{1,0:T(8,128)}, u32[]{:S(2)}) copy-start(f32[512,768]{1,0:T(8,128)} %get-tuple-element.31) | copy-start | bytes 4718596
  194.6 9.4 %copy-start.56 = (f32[512]{0:T(512)S(1)}, f32[512]{0:T(512)}, u32[]{:S(2)}) copy-start(f32[512]{0:T(512)} %copy-done.55) | copy-start | bytes 6148
  194.6 23.7 %all-to-all-start.2 = ((bf16[4,2,128,768]{3,2,1,0:T(8,128)(2,1)}), bf16[4,2,128,768]{3,2,1,0:T(8,128)(2,1)S(1)}, u32[]{:S(2)}, u32[]{:S(2)}) async-start(bf16[4,2,128,768]{3,2,1,0:T(8,128)(2,1)} %bitcast.234), calls=%async_computation.2 | async-start | bytes 3145728 | tf_op jit(solution)/shard_map/all_to_all | solution.py:1046
  199.1 7.8 %copy-start.58 = (bf16[2,768,2]{1,2,0:T(2,128)(2,1)S(1)}, bf16[2,768,2]{1,2,0:T(2,128)(2,1)}, u32[]{:S(2)}) copy-start(bf16[2,768,2]{1,2,0:T(2,128)(2,1)} %param.39) | copy-start | bytes 18436
  206.3 20.5 %copy-start.64 = (f32[512]{0:T(512)}, f32[512]{0:T(512)S(1)}, u32[]{:S(2)}) copy-start(f32[512]{0:T(512)S(1)} %get-tuple-element.98) | copy-start | bytes 6148
  206.3 20.5 %copy-start.66 = (f32[512]{0:T(512)}, f32[512]{0:T(512)S(1)}, u32[]{:S(2)}) copy-start(f32[512]{0:T(512)S(1)} %get-tuple-element.101) | copy-start | bytes 6148
  210.8 15.9 %copy-start.29 = (bf16[4,2,16,768]{3,0,2,1:T(4,128)(2,1)S(1)}, bf16[4,2,16,768]{3,0,2,1:T(4,128)(2,1)}, u32[]{:S(2)}) copy-start(bf16[4,2,16,768]{3,0,2,1:T(4,128)(2,1)} %convolution_convert_fusion.4) | copy-start | bytes 589828
  210.8 16.4 %copy-start.40 = (bf16[4,2,2048,16]{2,0,3,1:T(4,128)(2,1)S(1)}, bf16[4,2,2048,16]{2,0,3,1:T(4,128)(2,1)}, u32[]{:S(2)}) copy-start(bf16[4,2,2048,16]{2,0,3,1:T(4,128)(2,1)} %convolution_convert_fusion.1) | copy-start | bytes 1572868
  227.3 11.1 %copy-start.45 = (bf16[4,2,128,32]{2,3,1,0:T(8,128)(2,1)S(1)}, bf16[4,2,128,32]{2,3,1,0:T(8,128)(2,1)}, u32[]{:S(2)}) copy-start(bf16[4,2,128,32]{2,3,1,0:T(8,128)(2,1)} %copy-done.44) | copy-start | bytes 196612
  270.8 24.8 %all-to-all-start.3 = ((bf16[4,2,128,768]{3,2,1,0:T(8,128)(2,1)}), bf16[4,2,128,768]{3,2,1,0:T(8,128)(2,1)}, u32[]{:S(2)}, u32[]{:S(2)}) async-start(bf16[4,2,128,768]{3,2,1,0:T(8,128)(2,1)} %copy.292), calls=%async_computation.3 | async-start | bytes 3145728 | tf_op jit(solution)/shard_map/all_to_all | solution.py:1048
  282.0 15.2 %copy-start.53 = (s32[1024]{0:T(1024)S(1)}, s32[1024]{0:T(1024)}, u32[]{:S(2)}) copy-start(s32[1024]{0:T(1024)} %copy-done.52) | copy-start | bytes 12292
  307.8 14.7 %copy-start.4 = (f32[512,768]{1,0:T(8,128)S(1)}, f32[512,768]{1,0:T(8,128)}, u32[]{:S(2)}) copy-start(f32[512,768]{1,0:T(8,128)} %get-tuple-element.31) | copy-start | bytes 4718596
  307.8 14.7 %copy-start.11 = (bf16[1,512,768]{2,1,0:T(8,128)(2,1)S(1)}, bf16[1,512,768]{2,1,0:T(8,128)(2,1)}, u32[]{:S(2)}) copy-start(bf16[1,512,768]{2,1,0:T(8,128)(2,1)} %param.47) | copy-start | bytes 2359300
  307.8 14.7 %copy-start.14 = (f32[512,768]{1,0:T(8,128)S(1)}, f32[512,768]{1,0:T(8,128)}, u32[]{:S(2)}) copy-start(f32[512,768]{1,0:T(8,128)} %fusion.124) | copy-start | bytes 4718596
  307.8 14.7 %copy-start.15 = (f32[512,768]{1,0:T(8,128)S(1)}, f32[512,768]{1,0:T(8,128)}, u32[]{:S(2)}) copy-start(f32[512,768]{1,0:T(8,128)} %fusion.107) | copy-start | bytes 4718596
  307.8 14.7 %copy-start.59 = (bf16[2,768,2]{1,2,0:T(2,128)(2,1)S(1)}, bf16[2,768,2]{1,2,0:T(2,128)(2,1)}, u32[]{:S(2)}) copy-start(bf16[2,768,2]{1,2,0:T(2,128)(2,1)} %param.39) | copy-start | bytes 18436
  307.8 14.7 %copy-start.65 = (f32[512]{0:T(512)S(1)}, f32[512]{0:T(512)}, u32[]{:S(2)}) copy-start(f32[512]{0:T(512)} %copy-done.64) | copy-start | bytes 6148
  307.9 14.7 %copy-start.67 = (f32[512]{0:T(512)S(1)}, f32[512]{0:T(512)}, u32[]{:S(2)}) copy-start(f32[512]{0:T(512)} %copy-done.66) | copy-start | bytes 6148
  307.9 14.7 %copy-start.69 = (f32[512]{0:T(512)S(1)}, f32[512]{0:T(512)}, u32[]{:S(2)}) copy-start(f32[512]{0:T(512)} %copy-done.68) | copy-start | bytes 6148
  307.9 14.7 %copy-start.71 = (f32[512]{0:T(512)S(1)}, f32[512]{0:T(512)}, u32[]{:S(2)}) copy-start(f32[512]{0:T(512)} %copy-done.70) | copy-start | bytes 6148
  307.9 14.7 %copy-start.73 = (f32[512]{0:T(512)S(1)}, f32[512]{0:T(512)}, u32[]{:S(2)}) copy-start(f32[512]{0:T(512)} %get-tuple-element.104) | copy-start | bytes 6148
  307.9 14.7 %copy-start.74 = (f32[512,1]{0,1:T(1,128)S(1)}, f32[512,1]{0,1:T(1,128)}, u32[]{:S(2)}) copy-start(f32[512,1]{0,1:T(1,128)} %slice.154) | copy-start | bytes 6148
  307.9 14.7 %copy-start.75 = (f32[512,1]{0,1:T(1,128)S(1)}, f32[512,1]{0,1:T(1,128)}, u32[]{:S(2)}) copy-start(f32[512,1]{0,1:T(1,128)} %slice.157) | copy-start | bytes 6148
  307.9 14.7 %copy-start.76 = (f32[512]{0:T(512)S(1)}, f32[512]{0:T(512)}, u32[]{:S(2)}) copy-start(f32[512]{0:T(512)} %get-tuple-element.108) | copy-start | bytes 6148
  542.9 8.8 %copy-start.30 = (f32[512,768]{1,0:T(8,128)S(1)}, f32[512,768]{1,0:T(8,128)}, u32[]{:S(2)}) copy-start(f32[512,768]{1,0:T(8,128)} %get-tuple-element.43) | copy-start | bytes 4718596
  542.9 9.9 %copy-start.1 = (bf16[8,2,2048,16]{2,3,1,0:T(8,128)(2,1)S(1)}, bf16[8,2,2048,16]{2,3,1,0:T(8,128)(2,1)}, u32[]{:S(2)}) copy-start(bf16[8,2,2048,16]{2,3,1,0:T(8,128)(2,1)} %param.45) | copy-start | bytes 3145732
  (42 other events, 158.5 us)
